TPU v7x, 256 devices: a whole 4x4x8 slice. The times are simulated.
256 devices in a mesh: gx: 64 (over z_lo, x, y), gy: 4 (over z_hi, core).
Axes of the slice: x: 4, y: 4, z: 8 (z_hi: 2, z_lo: 4; z = z_hi * 4 + z_lo), core: 2. Of those that a mesh axis runs over, the one named last changes fastest.
Arguments:
- positions: float32 [3, 16384], P(None, ('gx', 'gy')), may hold values from 0 to 22.4, as said below
- features: bfloat16 [64, 16384], P(None, ('gx', 'gy')), may hold values from -6 to 6
- send_list: int32 [8192], P(('gx', 'gy')), may hold values from 0 to 63, as said below
- edge_src: int32 [262144], P(('gx', 'gy')), may hold values from 0 to 319, as said below
- edge_dst: int32 [262144], P(('gx', 'gy')), may hold values from 0 to 63, as said below
- edge_count: int32 [256], P(('gx', 'gy')), may hold values from 128 to 1024, as said below
- w_embed: float32 [136, 64], replicated, may hold values from -0.5 to 0.5
- w_env: float32 [2, 64, 192], replicated, may hold values from -0.75 to 0.75
- w_update: float32 [2, 256, 64], replicated, may hold values from -0.375 to 0.375
- w_out: float32 [64], replicated, may hold values from -0.75 to 0.75
Outputs:
- forces: float32 [3, 16384], P(None, ('gx', 'gy'))
- energy: float32 [], replicated
Inputs may be any that keep to these rules, and one draw needn't show every extreme that they name: `positions`: x and y lie within the device's cell of width 6; z lies within the slab. `send_list`: each device's 32 entries are distinct owned slots in increasing order. `edge_src`: indices into the device's table of 64 own atoms and 8 ghost blocks. `edge_dst`: owned slots of the device. `edge_count`: each device's count is a multiple of 128; some device has all 1024 slots live in every draw.
All inputs are finite; a program needn't handle non-finite values.
Results may differ from a plain program's by a relative error of at most 0.00035.
Values sent between devices are 32-bit elements; how exact they have to be, the bound alone decides.
A program may use at most 64 MiB of HBM per device.

v0:
```python
import math

import jax
import jax.numpy as jnp
from jax import lax
from jax.experimental import pallas as pl
from jax.experimental.pallas import tpu as pltpu
from jax.sharding import PartitionSpec as P

C = 64
NB = 8
LAYERS = 2
ATOMS = 64
GHOST = 32
EDGES = 1024
SCALE = 16 ** (-0.5)
OFFSETS = ((-1, -1), (-1, 0), (-1, 1), (0, -1), (0, 1), (1, -1), (1, 0), (1, 1))
WIDTH = 6.0
CUTOFF = 5.0
SPAN = ((0, 64), (64, 256), (256, 576))
F32 = jnp.float32
BF16 = jnp.bfloat16
MESH = pl.DeviceIdType.MESH


def split(x):
    hi = x.astype(BF16)
    return hi, (x - hi.astype(F32)).astype(BF16)


def split3(x):
    hi = x.astype(BF16)
    rest = x - hi.astype(F32)
    mid = rest.astype(BF16)
    return hi, mid, (rest - mid.astype(F32)).astype(BF16)


def dot(x, y):
    return lax.dot_general(x, y, (((1,), (0,)), ((), ())), preferred_element_type=F32)


def dot_t(x, y):
    return lax.dot_general(x, y, (((1,), (1,)), ((), ())), preferred_element_type=F32)


def mul3(x, y, product=dot):
    return product(x[0], y[0]) + product(x[1], y[0]) + product(x[0], y[1])


def row_of(v):
    return jnp.concatenate([v[j : j + 1, :] for j in range(8)], axis=1)


def pick_lane(tables, index):
    lane = index & 127
    which = index >> 7
    result = None
    for t, table in enumerate(tables):
        wide = jnp.broadcast_to(table, (8, 128))
        got = jnp.take_along_axis(wide, lane, axis=1, mode="promise_in_bounds")
        result = got if result is None else jnp.where(which == t, got, result)
    return result


def silu_pair(q):
    s = 1.0 / (1.0 + jnp.exp(-q))
    value = q * s
    return value, s + value * (1.0 - s)


def phases_of(columns, rows):
    phases = []
    stride = 1
    while stride < columns:
        size = 4 if (columns // stride) % 4 == 0 else columns // stride
        phases.append(("gx", stride, size))
        stride *= size
    phases.append(("gy", 1, rows))
    return phases


def kernel(
    columns, rows, phases,
    pos_ref, feat_ref, send_ref, src_ref, dst_ref, count_ref, we_ref, wv_ref, wu_ref, wo_ref,
    forces_ref, energy_ref,
    pay, table, ah, al, oh, vh, vl, gsrc, gbuf, ebuf,
    send_sem, recv_sem, gsend_sem, grecv_sem, esend_sem, erecv_sem,
):
    a = lax.axis_index("gx")
    b = lax.axis_index("gy")

    def peer(k):
        dx, dy = OFFSETS[k]
        return (lax.rem(a + dx + columns, columns), b + dy)

    def when_valid(k, act, otherwise=None):
        dy = OFFSETS[k][1]
        if dy == 0:
            act()
            return
        good = (b > 0) if dy < 0 else (b < rows - 1)
        pl.when(good)(act)
        if otherwise is not None:
            pl.when(jnp.logical_not(good))(otherwise)

    def member(ph):
        axis, stride, size = phases[ph]
        index = a if axis == "gx" else b
        return lax.rem(index // stride, size)

    def energy_peer(ph, t):
        axis, stride, size = phases[ph]
        me = member(ph)
        step = (lax.rem(me + t, size) - me) * stride
        return (a + step, b) if axis == "gx" else (a, b + step)

    barrier = pltpu.get_barrier_semaphore()
    for k in range(8):
        when_valid(k, lambda k=k: pl.semaphore_signal(barrier, inc=1, device_id=peer(k), device_id_type=MESH))
    greeted = 0
    for ph in range(len(phases)):
        for t in range(1, phases[ph][2]):
            pl.semaphore_signal(barrier, inc=1, device_id=energy_peer(ph, t), device_id_type=MESH)
            greeted += 1

    we_hi, we_lo = split(we_ref[0 : 2 * C, :].T)
    we_both = jnp.concatenate(
        [jnp.concatenate([we_hi[:, 0:C], we_lo[:, 0:C]], axis=1),
         jnp.concatenate([we_hi[:, C : 2 * C], we_lo[:, C : 2 * C]], axis=1)], axis=0)
    feat = feat_ref[...]
    own = dot(we_both, jnp.concatenate([feat, feat], axis=0))
    own_src, own_dst = own[0:C], own[C : 2 * C]
    pos = pos_ref[...]
    send4 = jnp.concatenate([send_ref[...]] * 4, axis=1)
    st4 = (lax.broadcasted_iota(jnp.int32, (ATOMS, 128), 0) == send4).astype(F32).astype(BF16)
    exported = jnp.concatenate([own_src, pos, jnp.zeros((61, ATOMS), F32)], axis=0)
    e3 = split3(jnp.concatenate([exported, jnp.zeros((128, 128 - ATOMS), F32)], axis=1))
    st4_tall = jnp.concatenate([st4, jnp.zeros((128 - ATOMS, 128), BF16)], axis=0)
    payload = (dot(e3[2], st4_tall) + dot(e3[1], st4_tall)) + dot(e3[0], st4_tall)
    pay[...] = payload.T[0:GHOST, :]

    inner = jnp.logical_and(b > 0, b < rows - 1)
    pl.semaphore_wait(barrier, greeted + jnp.where(inner, 8, 5))

    def ghost_copy(k):
        return pltpu.make_async_remote_copy(
            src_ref=pay, dst_ref=table.at[7 - k], send_sem=send_sem.at[k], recv_sem=recv_sem.at[7 - k],
            device_id=peer(k), device_id_type=MESH,
        )

    for k in range(8):
        when_valid(k, lambda k=k: ghost_copy(k).start())

    src = src_ref[...]
    dst = dst_ref[...]
    block = (src - ATOMS) >> 5
    ghost = src >= ATOMS
    ox = jnp.zeros((8, 128), F32)
    oy = jnp.zeros((8, 128), F32)
    for k, (dx, dy) in enumerate(OFFSETS):
        here = jnp.logical_and(ghost, block == k)
        if dx:
            ox = jnp.where(here, WIDTH * dx, ox)
        if dy:
            oy = jnp.where(here, WIDTH * dy, oy)
    step_y = (oy * (1.0 / WIDTH)).astype(jnp.int32)
    reach = jnp.logical_and(b + step_y >= 0, b + step_y < rows)
    place = lax.broadcasted_iota(jnp.int32, (8, 128), 0) * 128 + lax.broadcasted_iota(jnp.int32, (8, 128), 1)
    live = jnp.where(jnp.logical_and(place < count_ref[...], reach), 1.0, 0.0)
    slot = jnp.where(ghost, src - ATOMS, src + 8 * GHOST)
    slot_row = row_of(slot)
    dst_row = row_of(dst)
    oh[0:320, :] = (lax.broadcasted_iota(jnp.int32, (320, EDGES), 0) == slot_row).astype(F32).astype(BF16)
    mask = lax.broadcasted_iota(jnp.int32, (ATOMS, EDGES), 0) == dst_row
    hot = mask.astype(F32).astype(BF16)
    oh[320:384, :] = hot
    ah[0:64, :] = hot
    al[0:64, :] = jnp.zeros((64, EDGES), BF16)
    pre_own = dot(jnp.concatenate(split(jnp.concatenate([own_src, own_dst], axis=1)), axis=0), oh[256:384, :])
    pre_own = pre_own[0:C] + pre_own[C : 2 * C]

    back_lhs, back_rhs, fore_lhs, fore_rhs, w0, w0t = [], [], [], [], [], []
    zero = jnp.zeros((C, C), F32)
    for layer in range(LAYERS):
        rows_fl, rows_fr, rows_bl, rows_br = [], [], [], []
        for d in range(3):
            env_hi, env_lo = split(wv_ref[layer, :, d * C : (d + 1) * C])
            upd_hi, upd_lo = split(wu_ref[layer, (d + 1) * C : (d + 2) * C, :])
            mt = dot(jnp.concatenate([env_hi, env_hi, env_lo, env_lo], axis=1),
                     jnp.concatenate([upd_hi, upd_lo, upd_hi, upd_lo], axis=0)) * SCALE
            m = mt.T
            mh, ml = split(jnp.concatenate([m, m], axis=1))
            rows_fl.append((jnp.concatenate([mh, ml], axis=0), mh))
            th, tl = split(jnp.concatenate([mt, mt], axis=1))
            rows_bl.append((jnp.concatenate([th, tl], axis=0), th))
            wide = jnp.concatenate([mt, zero], axis=1)
            rows_fr.append(split(jnp.concatenate([wide, wide], axis=0)))
            wide = jnp.concatenate([zero, m], axis=1)
            rows_br.append(split(jnp.concatenate([wide, wide], axis=0)))
        fore_lhs.append(rows_fl)
        fore_rhs.append(rows_fr)
        back_lhs.append(rows_bl)
        back_rhs.append(rows_br)
        own_w = wu_ref[layer, 0:C, :]
        w0.append(own_w)
        w0t.append(own_w.T)
    wr = we_ref[2 * C : 2 * C + NB, :]
    wr_low = wr - wr.astype(BF16).astype(F32)
    wr4 = jnp.concatenate([wr, wr, wr_low, jnp.zeros((104, C), F32)], axis=0).T.astype(BF16)
    wr2 = jnp.concatenate([wr, wr_low], axis=0)
    wr2 = jnp.concatenate([wr2, wr2], axis=1).astype(BF16)
    diagonal = lax.broadcasted_iota(jnp.int32, (C, C), 0) == lax.broadcasted_iota(jnp.int32, (C, C), 1)
    wo = jnp.sum(jnp.where(diagonal, wo_ref[...], 0.0), axis=1, keepdims=True)

    def blank(k):
        table[k] = jnp.zeros((GHOST, 128), F32)
        gbuf[k] = jnp.zeros((8, 128), F32)

    for k in range(8):
        when_valid(k, lambda k=k: ghost_copy(7 - k).wait_recv(), lambda k=k: blank(k))

    ghosts = jnp.concatenate([table[0:4].reshape(128, 128).T, table[4:8].reshape(128, 128).T], axis=1)
    own_pos = jnp.concatenate([pos, jnp.zeros((3, 64), F32)], axis=1)
    diff = []
    for i in range(3):
        at_ghost = ghosts[C + i : C + i + 1, :]
        mine = own_pos[i : i + 1, :]
        at_src = pick_lane([at_ghost[:, 0:128], at_ghost[:, 128:256], mine], slot)
        if i < 2:
            at_src = at_src + (ox, oy)[i]
        diff.append(at_src - pick_lane([mine], dst))
    dist = jnp.sqrt(diff[0] * diff[0] + diff[1] * diff[1] + diff[2] * diff[2] + 1.0)
    inv = 1.0 / dist
    ux, uy, uz = (v * inv for v in diff)
    root = math.sqrt(3.0)
    harm = [ux, uy, uz, root * ux * uy, root * uy * uz, 0.5 * (3.0 * uz * uz - 1.0), root * ux * uz,
            0.5 * root * (ux * ux - uy * uy)]
    short = jnp.maximum(1.0 - (dist * dist) * (1.0 / CUTOFF**2), 0.0)
    envelope = short * short
    cut = row_of(live * envelope)
    gain = envelope * inv
    slope = (-4.0 / CUTOFF**2) * dist * short
    gain_slope = (slope - gain) * inv
    for m in range(8):
        row = row_of(harm[m])
        high = row.astype(BF16).astype(F32)
        low = row - high
        ah[64 * (m + 1) : 64 * (m + 2), :] = jnp.where(mask, high, 0.0).astype(BF16)
        al[64 * (m + 1) : 64 * (m + 2), :] = jnp.where(mask, low, 0.0).astype(BF16)

    order = (lax.broadcasted_iota(jnp.int32, (NB, EDGES), 0) + 1).astype(F32)
    turns = order * row_of(jnp.minimum(dist, CUTOFF) * (1.0 / CUTOFF))
    whole = jnp.floor(turns + 0.5)
    angle = (turns - whole) * math.pi
    odd = whole - 2.0 * jnp.floor(whole * 0.5)
    sign = 1.0 - 2.0 * odd
    sq = angle * angle
    sine = 1.0 / 39916800.0
    for c in (-1.0 / 362880.0, 1.0 / 5040.0, -1.0 / 120.0, 1.0 / 6.0, -1.0):
        sine = c + sq * sine
    sine = -(angle * sine) * sign
    cosine = 1.0 / 479001600.0
    for c in (-1.0 / 3628800.0, 1.0 / 40320.0, -1.0 / 720.0, 1.0 / 24.0, -0.5, 1.0):
        cosine = c + sq * cosine
    cosine = cosine * sign
    gain_row = row_of(gain)
    radial = sine * gain_row
    radial_low = radial - radial.astype(BF16).astype(F32)
    radial4 = jnp.concatenate([radial, radial_low, radial, jnp.zeros((104, EDGES), F32)], axis=0).astype(BF16)

    from_ghost = dot(jnp.concatenate(split(ghosts[0:C, :]), axis=0), oh[0:256, :])
    pre = pre_own + from_ghost[0:C] + from_ghost[C : 2 * C] + dot(wr4, radial4)
    value0, grad0 = silu_pair(pre)
    feats = [value0 * cut]
    values, grads, maps = [], [], []

    def environment(two):
        first = dot_t(ah[0:576, :], two)
        return first[0:64], first[64:576] + dot_t(al[64:576, :], two)

    def mixed(parts, lhs, rhs, own_w):
        flat, tall = [], []
        for d in range(3):
            lo, hi = SPAN[d]
            x = split(parts[0] if d == 0 else parts[1][lo - 64 : hi - 64])
            both = dot_t(lhs[d][0], x[0])
            flat.append(both[0:C] + both[C : 2 * C] + dot_t(lhs[d][1], x[1]))
            if d:
                tall.append(mul3(x, rhs[d]))
        return jnp.concatenate(flat + [own_w], axis=1), jnp.concatenate(tall, axis=0)

    def spread(flat):
        hi, lo = split(flat)
        both = dot(jnp.concatenate([hi, lo], axis=0), ah[...])
        return both[0:C] + both[C : 2 * C] + dot(hi, al[...])

    def keep(row, x):
        hi, lo = split(x)
        vh[row : row + C, :] = hi
        vl[row : row + C, :] = lo
        ah[576:640, :] = hi
        al[576:640, :] = lo
        return jnp.concatenate([hi, lo], axis=0)

    for layer in range(LAYERS):
        f = feats[-1]
        parts = environment(keep(192 - 128 * layer, f))
        flat, tall = mixed(parts, fore_lhs[layer], fore_rhs[layer], w0t[layer])
        maps.append(tall)
        q = spread(flat)
        value, grad = silu_pair(q)
        values.append(value)
        grads.append(grad)
        feats.append(f + value * cut)

    def energy_copy(ph, t):
        size = phases[ph][2]
        me = member(ph)
        return pltpu.make_async_remote_copy(
            src_ref=ebuf.at[ph, me], dst_ref=ebuf.at[ph, me], send_sem=esend_sem.at[ph, t],
            recv_sem=erecv_sem.at[ph, t], device_id=energy_peer(ph, t), device_id_type=MESH,
        )

    def energy_out(ph, x):
        ebuf[ph, member(ph)] = x
        for t in range(1, phases[ph][2]):
            energy_copy(ph, t).start()

    def energy_in(ph):
        size = phases[ph][2]
        for t in range(1, size):
            came = lax.rem(member(ph) + size - t, size)
            pltpu.make_async_remote_copy(
                src_ref=ebuf.at[ph, came], dst_ref=ebuf.at[ph, came], send_sem=esend_sem.at[ph, t],
                recv_sem=erecv_sem.at[ph, t], device_id=energy_peer(ph, t), device_id_type=MESH,
            ).wait_recv()
        total = ebuf[ph, 0]
        for t in range(1, size):
            total = total + ebuf[ph, t]
        return total

    live_row = row_of(live)
    df = wo * live_row
    per_edge = feats[LAYERS] * df
    folded = per_edge[0:8]
    for s in range(1, 8):
        folded = folded + per_edge[8 * s : 8 * s + 8]
    piece = folded[:, 0:128]
    for j in range(1, 8):
        piece = piece + folded[:, 128 * j : 128 * j + 128]
    energy_out(0, piece)
    last = len(phases) - 1
    done = 0

    dcut = jnp.zeros((1, EDGES), F32)
    uts = [None] * LAYERS
    for layer in reversed(range(LAYERS)):
        dcut = dcut + jnp.sum(df * values[layer], axis=0, keepdims=True)
        dq = df * cut * grads[layer]
        parts = environment(keep(128 - 128 * layer, dq))
        flat, tall = mixed(parts, back_lhs[layer], back_rhs[layer], w0[layer])
        uts[layer] = maps[layer] + tall
        df = df + spread(flat)
        if done < last:
            energy_out(done + 1, energy_in(done))
            done += 1
    dcut = dcut + jnp.sum(df * value0, axis=0, keepdims=True)
    dpre = df * cut * grad0
    both = dot(wr2, jnp.concatenate(split(dpre), axis=0))
    dradial = both[0:8] + both[8:16]
    steps = order * (math.pi / CUTOFF)
    dr = jnp.sum(dradial * (steps * cosine * gain_row + sine * row_of(gain_slope)), axis=0, keepdims=True)
    dr = dr + dcut * row_of(live * slope)
    ut = jnp.concatenate([uts[1], uts[0]], axis=1)
    uh, ul = split(ut)
    tiles = []
    for n in range(4):
        lanes = slice(256 * n, 256 * (n + 1))
        right = vh[:, lanes]
        part = dot(uh, right) + dot(ul, right) + dot(uh, vl[:, lanes])
        keep_here = mask[:, lanes]
        tiles.append([
            jnp.sum(jnp.where(keep_here, part[64 * m : 64 * (m + 1)], 0.0), axis=0, keepdims=True) for m in range(8)
        ])
    g = [jnp.concatenate([tiles[n][m] for n in range(4)], axis=1) for m in range(8)]
    while done < last:
        energy_out(done + 1, energy_in(done))
        done += 1
    xr, yr, zr, ir = row_of(ux), row_of(uy), row_of(uz), row_of(inv)
    dux = g[0] + root * (g[3] * yr + g[6] * zr + g[7] * xr)
    duy = g[1] + root * (g[3] * xr + g[4] * zr - g[7] * yr)
    duz = g[2] + root * (g[4] * yr + g[6] * xr) + 3.0 * g[5] * zr
    radial_part = dr - (dux * xr + duy * yr + duz * zr) * ir
    dd = jnp.concatenate(
        [dux * ir + radial_part * xr, duy * ir + radial_part * yr, duz * ir + radial_part * zr,
         jnp.zeros((5, EDGES), F32)], axis=0)
    dd_low = dd - dd.astype(BF16).astype(F32)
    scattered = dot_t(jnp.concatenate([dd, dd_low], axis=0).astype(BF16), oh[...])
    scattered = scattered[0:8] + scattered[8:16]
    gsrc[0] = scattered[:, 0:128]
    gsrc[1] = scattered[:, 128:256]

    def force_copy(k):
        return pltpu.make_async_remote_copy(
            src_ref=gsrc.at[k // 4], dst_ref=gbuf.at[7 - k], send_sem=gsend_sem.at[k], recv_sem=grecv_sem.at[7 - k],
            device_id=peer(k), device_id_type=MESH,
        )

    for k in range(8):
        when_valid(k, lambda k=k: force_copy(k).start())
    at_own = scattered[:, 256:320] - scattered[:, 320:384]
    for k in range(8):
        when_valid(k, lambda k=k: force_copy(7 - k).wait_recv())
    group = lax.broadcasted_iota(jnp.int32, (8, 128), 1) >> 5
    acc = jnp.zeros((8, 128), F32)
    for k in range(8):
        acc = acc + jnp.where(group == (7 - k) % 4, gbuf[k], 0.0)
    acc_low = acc - acc.astype(BF16).astype(F32)
    returned = dot_t(jnp.concatenate([acc, acc_low], axis=0).astype(BF16), st4)
    returned = returned[0:8] + returned[8:16]
    forces_ref[...] = -(at_own + returned)[0:3, :]

    total = energy_in(last)
    energy_ref[...] = jnp.sum(jnp.sum(total, axis=0, keepdims=True), axis=1, keepdims=True)

    for k in range(8):
        when_valid(k, lambda k=k: (ghost_copy(k).wait_send(), force_copy(k).wait_send())[0])
    for ph in range(len(phases)):
        for t in range(1, phases[ph][2]):
            energy_copy(ph, t).wait_send()


def solution(mesh):
    columns, rows = mesh.shape["gx"], mesh.shape["gy"]
    phases = phases_of(columns, rows)
    most = max(size for _, _, size in phases)

    def per_device(positions, features, send_list, edge_src, edge_dst, edge_count, w_embed, w_env, w_update, w_out):
        def body(*refs):
            kernel(columns, rows, phases, *refs)

        vmem = pl.BlockSpec(memory_space=pltpu.VMEM)
        forces, energy = pl.pallas_call(
            body,
            out_shape=(jax.ShapeDtypeStruct((3, ATOMS), F32), jax.ShapeDtypeStruct((1, 1), F32)),
            in_specs=[vmem] * 10,
            out_specs=(vmem, vmem),
            scratch_shapes=[
                pltpu.VMEM((GHOST, 128), F32),
                pltpu.VMEM((8, GHOST, 128), F32),
                pltpu.VMEM((640, EDGES), BF16),
                pltpu.VMEM((640, EDGES), BF16),
                pltpu.VMEM((384, EDGES), BF16),
                pltpu.VMEM((256, EDGES), BF16),
                pltpu.VMEM((256, EDGES), BF16),
                pltpu.VMEM((2, 8, 128), F32),
                pltpu.VMEM((8, 8, 128), F32),
                pltpu.VMEM((len(phases), most, 8, 128), F32),
                pltpu.SemaphoreType.DMA((8,)),
                pltpu.SemaphoreType.DMA((8,)),
                pltpu.SemaphoreType.DMA((8,)),
                pltpu.SemaphoreType.DMA((8,)),
                pltpu.SemaphoreType.DMA((len(phases), most)),
                pltpu.SemaphoreType.DMA((len(phases), most)),
            ],
            compiler_params=pltpu.CompilerParams(
                collective_id=0, has_side_effects=True, vmem_limit_bytes=40 * 1024 * 1024
            ),
        )(
            positions, features, send_list.reshape(1, GHOST), edge_src.reshape(8, 128), edge_dst.reshape(8, 128),
            edge_count.reshape(1, 1), w_embed, w_env, w_update, w_out.reshape(1, C),
        )
        return forces, energy.reshape(())

    placed = (
        P(None, ("gx", "gy")), P(None, ("gx", "gy")), P(("gx", "gy")), P(("gx", "gy")), P(("gx", "gy")),
        P(("gx", "gy")), P(), P(), P(), P(),
    )
    return jax.shard_map(
        per_device, mesh=mesh, in_specs=placed, out_specs=(P(None, ("gx", "gy")), P()), check_vma=False
    )
```

profile of v0, /device:TPU:1, one launch (start us, length us, event | category | flops | bytes accessed | tf_op | source)
XLA Modules:
  0.0 47.0 jit_solution(1911908433429311581)
XLA Ops:
  0.6 0.0 copy-start.7
  1.3 0.9 %copy.12.refs_6_ = f32[136,64]{1,0:T(8,128)S(1)} copy(f32[136,64]{0,1:T(8,128)} %param.16) | data formatting | bytes 69632 | tf_op args[6]
  2.3 0.0 copy-done.7
  2.3 0.0 copy-start
  2.3 0.0 copy-start.1
  2.3 0.0 copy-start.2
  2.3 0.0 copy-start.3
  2.3 0.0 copy-start.4
  2.3 0.0 copy-start.5
  2.3 0.0 copy-start.6
  2.4 0.1 copy.13.refs_8_
  2.5 0.7 %copy-done = f32[2,64,192]{2,1,0:T(8,128)S(1)} copy-done((f32[2,64,192]{2,1,0:T(8,128)S(1)}, f32[2,64,192]{2,1,0:T(8,128)}, u32[]{:S(2)}) %copy-start) | copy-done | bytes 98328
  3.2 0.0 copy-done.1
  3.2 0.0 copy-done.2
  3.2 0.0 copy-done.3
  3.2 0.0 copy-done.4
  3.2 0.0 copy-done.5
  3.2 0.0 copy-done.6
  3.2 41.4 %shard_map.113 = (f32[3,64]{1,0:T(4,128)S(1)}, f32[1,1]{1,0:T(1,128)}) custom-call(f32[3,64]{1,0:T(4,128)S(1)} %copy-done.4, bf16[64,64]{1,0:T(8,128)(2,1)S(1)} %copy-done.1, s32[1,32]{1,0:T(1,128)S(1)} %bitcast.9, s32[8,128]{1,0:T(8,128)S(1)} %bitcast.7, s32[8,128]{1,0:T(8,128)S(1)} %bitcast.8, s32[1,1]{1,0:T(1,128)} %bitcast.6.refs_5_, ...), custom_call_target="tpu_custom_call" | custom-call | tf_op jit(solution)/shard_map/pallas_call | solution.py:443
  44.6 0.6 %copy.17 = f32[3,64]{1,0:T(4,128)} copy(f32[3,64]{1,0:T(4,128)S(1)} %get-tuple-element.8) | data formatting | bytes 1536
Async XLA Ops:
  0.6 1.6 %copy-start.7 = (f32[2,256,64]{1,2,0:T(8,128)S(1)}, f32[2,256,64]{1,2,0:T(8,128)}, u32[]{:S(2)}) copy-start(f32[2,256,64]{1,2,0:T(8,128)} %param.18) | copy-start | bytes 393220
  2.3 0.9 %copy-start = (f32[2,64,192]{2,1,0:T(8,128)S(1)}, f32[2,64,192]{2,1,0:T(8,128)}, u32[]{:S(2)}) copy-start(f32[2,64,192]{2,1,0:T(8,128)} %refs_7_.1) | copy-start | bytes 294916
  2.3 0.9 %copy-start.1 = (bf16[64,64]{1,0:T(8,128)(2,1)S(1)}, bf16[64,64]{1,0:T(8,128)(2,1)}, u32[]{:S(2)}) copy-start(bf16[64,64]{1,0:T(8,128)(2,1)} %refs_1_.1) | copy-start | bytes 24580
  2.3 0.9 %copy-start.2 = (s32[1024]{0:T(1024)S(1)}, s32[1024]{0:T(1024)}, u32[]{:S(2)}) copy-start(s32[1024]{0:T(1024)} %param.13) | copy-start | bytes 12292
  2.3 0.9 %copy-start.3 = (s32[1024]{0:T(1024)S(1)}, s32[1024]{0:T(1024)}, u32[]{:S(2)}) copy-start(s32[1024]{0:T(1024)} %param.14) | copy-start | bytes 12292
  2.3 0.9 %copy-start.4 = (f32[3,64]{1,0:T(4,128)S(1)}, f32[3,64]{1,0:T(4,128)}, u32[]{:S(2)}) copy-start(f32[3,64]{1,0:T(4,128)} %refs_0_.1) | copy-start | bytes 2308
  2.3 0.9 %copy-start.5 = (s32[32]{0:T(128)S(1)}, s32[32]{0:T(128)}, u32[]{:S(2)}) copy-start(s32[32]{0:T(128)} %param.12) | copy-start | bytes 388
  2.3 0.9 %copy-start.6 = (f32[64]{0:T(128)S(1)}, f32[64]{0:T(128)}, u32[]{:S(2)}) copy-start(f32[64]{0:T(128)} %param.19) | copy-start | bytes 772
where the time goes:
time: 47.2 us; the launch traced here: 47 us
  Pallas kernels  41.4 us (88%)
  between operations  3.23 us (7%)
  local copies, waits for them, and re-layouts  2.38 us (5%)
    pallas_call x1, Pallas kernels, per_device(): pl.pallas_call(body, out_shape=(jax.ShapeDtypeStruct((3, ATOMS), F32), ja...  41.4 us
    unnamed x19, local copies, waits for them, and re-layouts  2.38 us

commit v1 on v0

--- a/solution.py
+++ b/solution.py
@@ -21,6 +21,8 @@
 F32 = jnp.float32
 BF16 = jnp.bfloat16
 MESH = pl.DeviceIdType.MESH
+TILE = 256
+CUT, LIVE, UX, UY, UZ, INV, DIST, GAIN, BEND, SLOPE, DCUT = 0, 1, 2, 3, 4, 5, 6, 7, 8, 9, 10
 
 
 def split(x):
@@ -45,10 +47,6 @@
 
 def mul3(x, y, product=dot):
     return product(x[0], y[0]) + product(x[1], y[0]) + product(x[0], y[1])
-
-
-def row_of(v):
-    return jnp.concatenate([v[j : j + 1, :] for j in range(8)], axis=1)
 
 
 def pick_lane(tables, index):
@@ -62,12 +60,6 @@
     return result
 
 
-def silu_pair(q):
-    s = 1.0 / (1.0 + jnp.exp(-q))
-    value = q * s
-    return value, s + value * (1.0 - s)
-
-
 def phases_of(columns, rows):
     phases = []
     stride = 1
@@ -81,10 +73,11 @@
 
 def kernel(
     columns, rows, phases,
+    pos_in, feat_in, send_in, src_in, dst_in, count_in, we_in, wv_in, wu_in, wo_in,
+    forces_ref, energy_ref,
     pos_ref, feat_ref, send_ref, src_ref, dst_ref, count_ref, we_ref, wv_ref, wu_ref, wo_ref,
-    forces_ref, energy_ref,
-    pay, table, ah, al, oh, vh, vl, gsrc, gbuf, ebuf,
-    send_sem, recv_sem, gsend_sem, grecv_sem, esend_sem, erecv_sem,
+    pay, table, ah, al, oh, vh, vl, two, row, value, gain_cut, df, dradial_map, ddb, gsrc, gbuf, ebuf,
+    in_sem, send_sem, recv_sem, gsend_sem, grecv_sem, esend_sem, erecv_sem,
 ):
     a = lax.axis_index("gx")
     b = lax.axis_index("gy")
@@ -123,7 +116,18 @@
             pl.semaphore_signal(barrier, inc=1, device_id=energy_peer(ph, t), device_id_type=MESH)
             greeted += 1
 
-    we_hi, we_lo = split(we_ref[0 : 2 * C, :].T)
+    fetched = [
+        pltpu.make_async_copy(given, held, in_sem.at[i])
+        for i, (given, held) in enumerate([
+            (pos_in, pos_ref), (feat_in, feat_ref), (send_in, send_ref), (we_in, we_ref), (src_in, src_ref),
+            (dst_in, dst_ref), (count_in, count_ref), (wv_in, wv_ref), (wu_in, wu_ref), (wo_in, wo_ref)])
+    ]
+    for copy in fetched:
+        copy.start()
+    for copy in fetched[0:4]:
+        copy.wait()
+
+    we_hi, we_lo = split(we_ref[:, 0 : 2 * C])
     we_both = jnp.concatenate(
         [jnp.concatenate([we_hi[:, 0:C], we_lo[:, 0:C]], axis=1),
          jnp.concatenate([we_hi[:, C : 2 * C], we_lo[:, C : 2 * C]], axis=1)], axis=0)
@@ -150,6 +154,19 @@
 
     for k in range(8):
         when_valid(k, lambda k=k: ghost_copy(k).start())
+    for copy in fetched[4:]:
+        copy.wait()
+
+    def put_row(i, v):
+        for j in range(8):
+            row[i : i + 1, 128 * j : 128 * (j + 1)] = v[j : j + 1, :]
+
+    def lanes_of(n):
+        return slice(TILE * n, TILE * (n + 1))
+
+    def tiles(act):
+        for n in range(EDGES // TILE):
+            act(lanes_of(n))
 
     src = src_ref[...]
     dst = dst_ref[...]
@@ -167,17 +184,16 @@
     reach = jnp.logical_and(b + step_y >= 0, b + step_y < rows)
     place = lax.broadcasted_iota(jnp.int32, (8, 128), 0) * 128 + lax.broadcasted_iota(jnp.int32, (8, 128), 1)
     live = jnp.where(jnp.logical_and(place < count_ref[...], reach), 1.0, 0.0)
+    put_row(LIVE, live)
     slot = jnp.where(ghost, src - ATOMS, src + 8 * GHOST)
-    slot_row = row_of(slot)
-    dst_row = row_of(dst)
-    oh[0:320, :] = (lax.broadcasted_iota(jnp.int32, (320, EDGES), 0) == slot_row).astype(F32).astype(BF16)
-    mask = lax.broadcasted_iota(jnp.int32, (ATOMS, EDGES), 0) == dst_row
-    hot = mask.astype(F32).astype(BF16)
-    oh[320:384, :] = hot
-    ah[0:64, :] = hot
-    al[0:64, :] = jnp.zeros((64, EDGES), BF16)
-    pre_own = dot(jnp.concatenate(split(jnp.concatenate([own_src, own_dst], axis=1)), axis=0), oh[256:384, :])
-    pre_own = pre_own[0:C] + pre_own[C : 2 * C]
+    for j in range(8):
+        lanes = slice(128 * j, 128 * (j + 1))
+        oh[0:320, lanes] = (
+            lax.broadcasted_iota(jnp.int32, (320, 128), 0) == slot[j : j + 1, :]).astype(F32).astype(BF16)
+        hot = (lax.broadcasted_iota(jnp.int32, (ATOMS, 128), 0) == dst[j : j + 1, :]).astype(F32).astype(BF16)
+        oh[320:384, lanes] = hot
+        ah[0:64, lanes] = hot
+        al[0:64, lanes] = jnp.zeros((64, 128), BF16)
 
     back_lhs, back_rhs, fore_lhs, fore_rhs, w0, w0t = [], [], [], [], [], []
     zero = jnp.zeros((C, C), F32)
@@ -185,10 +201,10 @@
         rows_fl, rows_fr, rows_bl, rows_br = [], [], [], []
         for d in range(3):
             env_hi, env_lo = split(wv_ref[layer, :, d * C : (d + 1) * C])
-            upd_hi, upd_lo = split(wu_ref[layer, (d + 1) * C : (d + 2) * C, :])
-            mt = dot(jnp.concatenate([env_hi, env_hi, env_lo, env_lo], axis=1),
-                     jnp.concatenate([upd_hi, upd_lo, upd_hi, upd_lo], axis=0)) * SCALE
-            m = mt.T
+            upd_hi, upd_lo = split(wu_ref[layer, :, (d + 1) * C : (d + 2) * C])
+            m = dot_t(jnp.concatenate([upd_hi, upd_hi, upd_lo, upd_lo], axis=1),
+                      jnp.concatenate([env_hi, env_lo, env_hi, env_lo], axis=1)) * SCALE
+            mt = m.T
             mh, ml = split(jnp.concatenate([m, m], axis=1))
             rows_fl.append((jnp.concatenate([mh, ml], axis=0), mh))
             th, tl = split(jnp.concatenate([mt, mt], axis=1))
@@ -201,10 +217,11 @@
         fore_rhs.append(rows_fr)
         back_lhs.append(rows_bl)
         back_rhs.append(rows_br)
-        own_w = wu_ref[layer, 0:C, :]
-        w0.append(own_w)
-        w0t.append(own_w.T)
-    wr = we_ref[2 * C : 2 * C + NB, :]
+        own_w = wu_ref[layer, :, 0:C]
+        w0.append(own_w.T)
+        w0t.append(own_w)
+    wrt = we_ref[:, 2 * C : 2 * C + NB]
+    wr = jnp.concatenate([wrt, jnp.zeros((C, 128 - NB), F32)], axis=1).T[0:NB, :]
     wr_low = wr - wr.astype(BF16).astype(F32)
     wr4 = jnp.concatenate([wr, wr, wr_low, jnp.zeros((104, C), F32)], axis=0).T.astype(BF16)
     wr2 = jnp.concatenate([wr, wr_low], axis=0)
@@ -237,46 +254,73 @@
             0.5 * root * (ux * ux - uy * uy)]
     short = jnp.maximum(1.0 - (dist * dist) * (1.0 / CUTOFF**2), 0.0)
     envelope = short * short
-    cut = row_of(live * envelope)
     gain = envelope * inv
     slope = (-4.0 / CUTOFF**2) * dist * short
-    gain_slope = (slope - gain) * inv
+    put_row(DIST, jnp.minimum(dist, CUTOFF) * (1.0 / CUTOFF))
+    put_row(GAIN, gain)
+    put_row(BEND, (slope - gain) * inv)
+    put_row(CUT, live * envelope)
+    put_row(SLOPE, live * slope)
+    for i, v in ((UX, ux), (UY, uy), (UZ, uz), (INV, inv)):
+        put_row(i, v)
     for m in range(8):
-        row = row_of(harm[m])
-        high = row.astype(BF16).astype(F32)
-        low = row - high
-        ah[64 * (m + 1) : 64 * (m + 2), :] = jnp.where(mask, high, 0.0).astype(BF16)
-        al[64 * (m + 1) : 64 * (m + 2), :] = jnp.where(mask, low, 0.0).astype(BF16)
-
-    order = (lax.broadcasted_iota(jnp.int32, (NB, EDGES), 0) + 1).astype(F32)
-    turns = order * row_of(jnp.minimum(dist, CUTOFF) * (1.0 / CUTOFF))
-    whole = jnp.floor(turns + 0.5)
-    angle = (turns - whole) * math.pi
-    odd = whole - 2.0 * jnp.floor(whole * 0.5)
-    sign = 1.0 - 2.0 * odd
-    sq = angle * angle
-    sine = 1.0 / 39916800.0
-    for c in (-1.0 / 362880.0, 1.0 / 5040.0, -1.0 / 120.0, 1.0 / 6.0, -1.0):
-        sine = c + sq * sine
-    sine = -(angle * sine) * sign
-    cosine = 1.0 / 479001600.0
-    for c in (-1.0 / 3628800.0, 1.0 / 40320.0, -1.0 / 720.0, 1.0 / 24.0, -0.5, 1.0):
-        cosine = c + sq * cosine
-    cosine = cosine * sign
-    gain_row = row_of(gain)
-    radial = sine * gain_row
-    radial_low = radial - radial.astype(BF16).astype(F32)
-    radial4 = jnp.concatenate([radial, radial_low, radial, jnp.zeros((104, EDGES), F32)], axis=0).astype(BF16)
-
-    from_ghost = dot(jnp.concatenate(split(ghosts[0:C, :]), axis=0), oh[0:256, :])
-    pre = pre_own + from_ghost[0:C] + from_ghost[C : 2 * C] + dot(wr4, radial4)
-    value0, grad0 = silu_pair(pre)
-    feats = [value0 * cut]
-    values, grads, maps = [], [], []
-
-    def environment(two):
-        first = dot_t(ah[0:576, :], two)
-        return first[0:64], first[64:576] + dot_t(al[64:576, :], two)
+        for j in range(8):
+            lanes = slice(128 * j, 128 * (j + 1))
+            wide = jnp.broadcast_to(harm[m][j : j + 1, :], (16, 128))
+            high, low = split(wide)
+            hot = ah[0:64, lanes]
+            ah[64 * (m + 1) : 64 * (m + 2), lanes] = hot * jnp.concatenate([high] * 4, axis=0)
+            al[64 * (m + 1) : 64 * (m + 2), lanes] = hot * jnp.concatenate([low] * 4, axis=0)
+
+    emb_hi, emb_lo = split(jnp.concatenate([ghosts[0:C, :], own_src, own_dst], axis=1))
+    emb = jnp.concatenate(
+        [jnp.concatenate([emb_hi, wr4], axis=1), jnp.concatenate([emb_lo, jnp.zeros((C, 128), BF16)], axis=1)], axis=0)
+    order = (lax.broadcasted_iota(jnp.int32, (NB, TILE), 0) + 1).astype(F32)
+
+    def keep(lanes, place, x):
+        hi, lo = split(x)
+        vh[place : place + C, lanes] = hi
+        vl[place : place + C, lanes] = lo
+        ah[576:640, lanes] = hi
+        al[576:640, lanes] = lo
+        two[0:C, lanes] = hi
+        two[C : 2 * C, lanes] = lo
+
+    def activate(lanes, stage, q):
+        s = 1.0 / (1.0 + jnp.exp(-q))
+        v = q * s
+        cut = row[CUT : CUT + 1, lanes]
+        value[stage, :, lanes] = v
+        gain_cut[stage, :, lanes] = (s + v * (1.0 - s)) * cut
+        return v * cut
+
+    def embed(lanes):
+        turns = order * row[DIST : DIST + 1, lanes]
+        whole = jnp.floor(turns + 0.5)
+        angle = (turns - whole) * math.pi
+        sign = 1.0 - 2.0 * (whole - 2.0 * jnp.floor(whole * 0.5))
+        sq = angle * angle
+        sine = 1.0 / 39916800.0
+        for c in (-1.0 / 362880.0, 1.0 / 5040.0, -1.0 / 120.0, 1.0 / 6.0, -1.0):
+            sine = c + sq * sine
+        sine = -(angle * sine) * sign
+        cosine = 1.0 / 479001600.0
+        for c in (-1.0 / 3628800.0, 1.0 / 40320.0, -1.0 / 720.0, 1.0 / 24.0, -0.5, 1.0):
+            cosine = c + sq * cosine
+        cosine = cosine * sign
+        near = row[GAIN : GAIN + 1, lanes]
+        radial = sine * near
+        dradial_map[:, lanes] = order * (math.pi / CUTOFF) * cosine * near + sine * row[BEND : BEND + 1, lanes]
+        low = radial - radial.astype(BF16).astype(F32)
+        oh[384:512, lanes] = jnp.concatenate([radial, low, radial, jnp.zeros((104, TILE), F32)], axis=0).astype(BF16)
+        both = dot(emb, oh[:, lanes])
+        f = activate(lanes, 0, both[0:C] + both[C : 2 * C])
+        df[:, lanes] = f
+        keep(lanes, 192, f)
+
+    def environment():
+        first = dot_t(ah[0:576, :], two[...])
+        return first[0:64], first[64:576] + dot_t(al[64:576, :], two[...])
 
     def mixed(parts, lhs, rhs, own_w):
         flat, tall = [], []
@@ -287,34 +331,14 @@
             flat.append(both[0:C] + both[C : 2 * C] + dot_t(lhs[d][1], x[1]))
             if d:
                 tall.append(mul3(x, rhs[d]))
-        return jnp.concatenate(flat + [own_w], axis=1), jnp.concatenate(tall, axis=0)
-
-    def spread(flat):
-        hi, lo = split(flat)
-        both = dot(jnp.concatenate([hi, lo], axis=0), ah[...])
-        return both[0:C] + both[C : 2 * C] + dot(hi, al[...])
-
-    def keep(row, x):
-        hi, lo = split(x)
-        vh[row : row + C, :] = hi
-        vl[row : row + C, :] = lo
-        ah[576:640, :] = hi
-        al[576:640, :] = lo
-        return jnp.concatenate([hi, lo], axis=0)
-
-    for layer in range(LAYERS):
-        f = feats[-1]
-        parts = environment(keep(192 - 128 * layer, f))
-        flat, tall = mixed(parts, fore_lhs[layer], fore_rhs[layer], w0t[layer])
-        maps.append(tall)
-        q = spread(flat)
-        value, grad = silu_pair(q)
-        values.append(value)
-        grads.append(grad)
-        feats.append(f + value * cut)
+        hi, lo = split(jnp.concatenate(flat + [own_w], axis=1))
+        return (jnp.concatenate([hi, lo], axis=0), hi), jnp.concatenate(tall, axis=0)
+
+    def spread(lanes, flat):
+        both = dot(flat[0], ah[:, lanes])
+        return both[0:C] + both[C : 2 * C] + dot(flat[1], al[:, lanes])
 
     def energy_copy(ph, t):
-        size = phases[ph][2]
         me = member(ph)
         return pltpu.make_async_remote_copy(
             src_ref=ebuf.at[ph, me], dst_ref=ebuf.at[ph, me], send_sem=esend_sem.at[ph, t],
@@ -339,67 +363,82 @@
             total = total + ebuf[ph, t]
         return total
 
-    live_row = row_of(live)
-    df = wo * live_row
-    per_edge = feats[LAYERS] * df
-    folded = per_edge[0:8]
-    for s in range(1, 8):
-        folded = folded + per_edge[8 * s : 8 * s + 8]
-    piece = folded[:, 0:128]
-    for j in range(1, 8):
-        piece = piece + folded[:, 128 * j : 128 * j + 128]
-    energy_out(0, piece)
     last = len(phases) - 1
-    done = 0
-
-    dcut = jnp.zeros((1, EDGES), F32)
-    uts = [None] * LAYERS
-    for layer in reversed(range(LAYERS)):
-        dcut = dcut + jnp.sum(df * values[layer], axis=0, keepdims=True)
-        dq = df * cut * grads[layer]
-        parts = environment(keep(128 - 128 * layer, dq))
-        flat, tall = mixed(parts, back_lhs[layer], back_rhs[layer], w0[layer])
-        uts[layer] = maps[layer] + tall
-        df = df + spread(flat)
-        if done < last:
-            energy_out(done + 1, energy_in(done))
-            done += 1
-    dcut = dcut + jnp.sum(df * value0, axis=0, keepdims=True)
-    dpre = df * cut * grad0
-    both = dot(wr2, jnp.concatenate(split(dpre), axis=0))
-    dradial = both[0:8] + both[8:16]
-    steps = order * (math.pi / CUTOFF)
-    dr = jnp.sum(dradial * (steps * cosine * gain_row + sine * row_of(gain_slope)), axis=0, keepdims=True)
-    dr = dr + dcut * row_of(live * slope)
-    ut = jnp.concatenate([uts[1], uts[0]], axis=1)
-    uh, ul = split(ut)
-    tiles = []
-    for n in range(4):
-        lanes = slice(256 * n, 256 * (n + 1))
+
+    tiles(embed)
+    flat, map0 = mixed(environment(), fore_lhs[0], fore_rhs[0], w0t[0])
+
+    def first_layer(lanes):
+        f = df[:, lanes] + activate(lanes, 1, spread(lanes, flat))
+        df[:, lanes] = f
+        keep(lanes, 64, f)
+
+    tiles(first_layer)
+    flat, map1 = mixed(environment(), fore_lhs[1], fore_rhs[1], w0t[1])
+    pieces = []
+
+    def turn(lanes):
+        q = spread(lanes, flat)
+        s = 1.0 / (1.0 + jnp.exp(-q))
+        v = q * s
+        cut = row[CUT : CUT + 1, lanes]
+        f = df[:, lanes] + v * cut
+        g = wo * row[LIVE : LIVE + 1, lanes]
+        per_edge = f * g
+        piece = per_edge[0:8]
+        for i in range(1, 8):
+            piece = piece + per_edge[8 * i : 8 * i + 8]
+        pieces.append(piece[:, 0:128] + piece[:, 128:256])
+        df[:, lanes] = g
+        row[DCUT : DCUT + 1, lanes] = jnp.sum(g * v, axis=0, keepdims=True)
+        keep(lanes, 0, g * ((s + v * (1.0 - s)) * cut))
+
+    tiles(turn)
+    energy_out(0, (pieces[0] + pieces[1]) + (pieces[2] + pieces[3]))
+
+    flat, tall = mixed(environment(), back_lhs[1], back_rhs[1], w0[1])
+    ut1 = map1 + tall
+
+    def back_first(lanes):
+        g = df[:, lanes] + spread(lanes, flat)
+        df[:, lanes] = g
+        row[DCUT : DCUT + 1, lanes] += jnp.sum(g * value[1, :, lanes], axis=0, keepdims=True)
+        keep(lanes, 128, g * gain_cut[1, :, lanes])
+
+    tiles(back_first)
+    for ph in range(0, min(1, last)):
+        energy_out(ph + 1, energy_in(ph))
+    flat, tall = mixed(environment(), back_lhs[0], back_rhs[0], w0[0])
+    for ph in range(1, min(2, last)):
+        energy_out(ph + 1, energy_in(ph))
+    uh, ul = split(jnp.concatenate([ut1, map0 + tall], axis=1))
+
+    def back_embed(lanes):
+        g = df[:, lanes] + spread(lanes, flat)
+        dcut = row[DCUT : DCUT + 1, lanes] + jnp.sum(g * value[0, :, lanes], axis=0, keepdims=True)
+        both = dot(wr2, jnp.concatenate(split(g * gain_cut[0, :, lanes]), axis=0))
+        dr = jnp.sum((both[0:8] + both[8:16]) * dradial_map[:, lanes], axis=0, keepdims=True)
+        dr = dr + dcut * row[SLOPE : SLOPE + 1, lanes]
         right = vh[:, lanes]
         part = dot(uh, right) + dot(ul, right) + dot(uh, vl[:, lanes])
-        keep_here = mask[:, lanes]
-        tiles.append([
-            jnp.sum(jnp.where(keep_here, part[64 * m : 64 * (m + 1)], 0.0), axis=0, keepdims=True) for m in range(8)
-        ])
-    g = [jnp.concatenate([tiles[n][m] for n in range(4)], axis=1) for m in range(8)]
-    while done < last:
-        energy_out(done + 1, energy_in(done))
-        done += 1
-    xr, yr, zr, ir = row_of(ux), row_of(uy), row_of(uz), row_of(inv)
-    dux = g[0] + root * (g[3] * yr + g[6] * zr + g[7] * xr)
-    duy = g[1] + root * (g[3] * xr + g[4] * zr - g[7] * yr)
-    duz = g[2] + root * (g[4] * yr + g[6] * xr) + 3.0 * g[5] * zr
-    radial_part = dr - (dux * xr + duy * yr + duz * zr) * ir
-    dd = jnp.concatenate(
-        [dux * ir + radial_part * xr, duy * ir + radial_part * yr, duz * ir + radial_part * zr,
-         jnp.zeros((5, EDGES), F32)], axis=0)
-    dd_low = dd - dd.astype(BF16).astype(F32)
-    scattered = dot_t(jnp.concatenate([dd, dd_low], axis=0).astype(BF16), oh[...])
+        hot = ah[0:64, lanes].astype(F32)
+        g = [jnp.sum(hot * part[64 * m : 64 * (m + 1)], axis=0, keepdims=True) for m in range(8)]
+        xr, yr, zr, ir = (row[i : i + 1, lanes] for i in (UX, UY, UZ, INV))
+        dux = g[0] + root * (g[3] * yr + g[6] * zr + g[7] * xr)
+        duy = g[1] + root * (g[3] * xr + g[4] * zr - g[7] * yr)
+        duz = g[2] + root * (g[4] * yr + g[6] * xr) + 3.0 * g[5] * zr
+        along = dr - (dux * xr + duy * yr + duz * zr) * ir
+        dd = jnp.concatenate(
+            [dux * ir + along * xr, duy * ir + along * yr, duz * ir + along * zr, jnp.zeros((5, TILE), F32)], axis=0)
+        ddb[:, lanes] = jnp.concatenate([dd, dd - dd.astype(BF16).astype(F32)], axis=0).astype(BF16)
+
+    tiles(back_embed)
+    for ph in range(2, last):
+        energy_out(ph + 1, energy_in(ph))
+    scattered = dot_t(ddb[...], oh[0:384, :])
     scattered = scattered[0:8] + scattered[8:16]
     gsrc[0] = scattered[:, 0:128]
     gsrc[1] = scattered[:, 128:256]
-
     def force_copy(k):
         return pltpu.make_async_remote_copy(
             src_ref=gsrc.at[k // 4], dst_ref=gbuf.at[7 - k], send_sem=gsend_sem.at[k], recv_sem=grecv_sem.at[7 - k],
@@ -440,22 +479,41 @@
             kernel(columns, rows, phases, *refs)
 
         vmem = pl.BlockSpec(memory_space=pltpu.VMEM)
+        anywhere = pl.BlockSpec(memory_space=pl.ANY)
         forces, energy = pl.pallas_call(
             body,
             out_shape=(jax.ShapeDtypeStruct((3, ATOMS), F32), jax.ShapeDtypeStruct((1, 1), F32)),
-            in_specs=[vmem] * 10,
+            in_specs=[anywhere] * 10,
             out_specs=(vmem, vmem),
             scratch_shapes=[
+                pltpu.VMEM((3, ATOMS), F32),
+                pltpu.VMEM((C, ATOMS), BF16),
+                pltpu.VMEM((1, GHOST), jnp.int32),
+                pltpu.VMEM((8, 128), jnp.int32),
+                pltpu.VMEM((8, 128), jnp.int32),
+                pltpu.VMEM((1, 1), jnp.int32),
+                pltpu.VMEM((C, 2 * C + NB), F32),
+                pltpu.VMEM((LAYERS, C, 3 * C), F32),
+                pltpu.VMEM((LAYERS, C, 4 * C), F32),
+                pltpu.VMEM((1, C), F32),
                 pltpu.VMEM((GHOST, 128), F32),
                 pltpu.VMEM((8, GHOST, 128), F32),
                 pltpu.VMEM((640, EDGES), BF16),
                 pltpu.VMEM((640, EDGES), BF16),
-                pltpu.VMEM((384, EDGES), BF16),
+                pltpu.VMEM((512, EDGES), BF16),
                 pltpu.VMEM((256, EDGES), BF16),
                 pltpu.VMEM((256, EDGES), BF16),
+                pltpu.VMEM((128, EDGES), BF16),
+                pltpu.VMEM((16, EDGES), F32),
+                pltpu.VMEM((2, C, EDGES), F32),
+                pltpu.VMEM((2, C, EDGES), F32),
+                pltpu.VMEM((C, EDGES), F32),
+                pltpu.VMEM((NB, EDGES), F32),
+                pltpu.VMEM((16, EDGES), BF16),
                 pltpu.VMEM((2, 8, 128), F32),
                 pltpu.VMEM((8, 8, 128), F32),
                 pltpu.VMEM((len(phases), most, 8, 128), F32),
+                pltpu.SemaphoreType.DMA((10,)),
                 pltpu.SemaphoreType.DMA((8,)),
                 pltpu.SemaphoreType.DMA((8,)),
                 pltpu.SemaphoreType.DMA((8,)),
@@ -464,11 +522,11 @@
                 pltpu.SemaphoreType.DMA((len(phases), most)),
             ],
             compiler_params=pltpu.CompilerParams(
-                collective_id=0, has_side_effects=True, vmem_limit_bytes=40 * 1024 * 1024
+                collective_id=0, has_side_effects=True, vmem_limit_bytes=60 * 1024 * 1024
             ),
         )(
             positions, features, send_list.reshape(1, GHOST), edge_src.reshape(8, 128), edge_dst.reshape(8, 128),
-            edge_count.reshape(1, 1), w_embed, w_env, w_update, w_out.reshape(1, C),
+            edge_count.reshape(1, 1), w_embed.T, w_env, jnp.swapaxes(w_update, 1, 2), w_out.reshape(1, C),
         )
         return forces, energy.reshape(())
 

time: 47.2 us -> 44.8 us (0.949)
  local copies, waits for them, and re-layouts: 2.38 us -> 1.22 us
  Pallas kernels: 41.4 us -> 40.4 us
    unnamed x19 -> x3, local copies, waits for them, and re-layouts: 2.38 us -> 1.22 us
    pallas_call x1, Pallas kernels: 41.4 us -> 40.4 us  [per_device(): pl.pallas_call(body, out_shape=(jax.ShapeDtypeStruct((3, ATOMS), F32), ja...]
where the time goes in v1:
time: 44.8 us; the launch traced here: 44.7 us
  Pallas kernels  40.4 us (90%)
  between operations  3.06 us (7%)
  local copies, waits for them, and re-layouts  1.22 us (3%)
    pallas_call x1, Pallas kernels, per_device(): pl.pallas_call(body, out_shape=(jax.ShapeDtypeStruct((3, ATOMS), F32), ja...  40.4 us
    unnamed x3, local copies, waits for them, and re-layouts  1.22 us

profile of v1, /device:TPU:1, one launch (start us, length us, event | category | flops | bytes accessed | tf_op | source)
XLA Modules:
  0.0 44.7 jit_solution(15316405463205960227)
XLA Ops:
  1.3 40.4 %shard_map.113 = (f32[3,64]{1,0:T(4,128)}, f32[1,1]{1,0:T(1,128)}) custom-call(f32[3,64]{1,0:T(4,128)} %refs_0_.1, bf16[64,64]{1,0:T(8,128)(2,1)} %refs_1_.1, s32[1,32]{1,0:T(1,128)} %bitcast.13, s32[8,128]{1,0:T(8,128)} %bitcast.11, s32[8,128]{1,0:T(8,128)} %bitcast.12, s32[1,1]{1,0:T(1,128)} %bitcast.8.refs_5_, f32[64,136]{1,0:T(8,128)} %bitcast.10, ...), custom_call_target="tpu_custom_call" | custom-call | tf_op jit(solution)/shard_map/pallas_call | solution.py:483
  41.7 0.0 copy-start
  41.7 0.6 %copy-done = f32[3,64]{1,0:T(4,128)S(1)} copy-done((f32[3,64]{1,0:T(4,128)S(1)}, f32[3,64]{1,0:T(4,128)}, u32[]{:S(2)}) %copy-start) | copy-done | bytes 792
  42.4 0.6 %copy.15 = f32[3,64]{1,0:T(4,128)} copy(f32[3,64]{1,0:T(4,128)S(1)} %copy-done) | data formatting | bytes 1536
Async XLA Ops:
  41.7 0.7 %copy-start = (f32[3,64]{1,0:T(4,128)S(1)}, f32[3,64]{1,0:T(4,128)}, u32[]{:S(2)}) copy-start(f32[3,64]{1,0:T(4,128)} %get-tuple-element.8) | copy-start | bytes 2308

commit v2 on v1

--- a/solution.py
+++ b/solution.py
@@ -17,7 +17,6 @@
 OFFSETS = ((-1, -1), (-1, 0), (-1, 1), (0, -1), (0, 1), (1, -1), (1, 0), (1, 1))
 WIDTH = 6.0
 CUTOFF = 5.0
-SPAN = ((0, 64), (64, 256), (256, 576))
 F32 = jnp.float32
 BF16 = jnp.bfloat16
 MESH = pl.DeviceIdType.MESH
@@ -43,10 +42,6 @@
 
 def dot_t(x, y):
     return lax.dot_general(x, y, (((1,), (1,)), ((), ())), preferred_element_type=F32)
-
-
-def mul3(x, y, product=dot):
-    return product(x[0], y[0]) + product(x[1], y[0]) + product(x[0], y[1])
 
 
 def pick_lane(tables, index):
@@ -76,7 +71,8 @@
     pos_in, feat_in, send_in, src_in, dst_in, count_in, we_in, wv_in, wu_in, wo_in,
     forces_ref, energy_ref,
     pos_ref, feat_ref, send_ref, src_ref, dst_ref, count_ref, we_ref, wv_ref, wu_ref, wo_ref,
-    pay, table, ah, al, oh, vh, vl, two, row, value, gain_cut, df, dradial_map, ddb, gsrc, gbuf, ebuf,
+    pay, table, ah, al, oh, vh, vl, row, value, gain_cut, df, dradial_map, ddb, lhs, own_weights, flat, kept, folded,
+    uth, utl, embs, gsrc, gbuf, ebuf,
     in_sem, send_sem, recv_sem, gsend_sem, grecv_sem, esend_sem, erecv_sem,
 ):
     a = lax.axis_index("gx")
@@ -161,12 +157,12 @@
         for j in range(8):
             row[i : i + 1, 128 * j : 128 * (j + 1)] = v[j : j + 1, :]
 
-    def lanes_of(n):
-        return slice(TILE * n, TILE * (n + 1))
+    def loop(count, act):
+        for i in range(count):
+            act(i)
 
     def tiles(act):
-        for n in range(EDGES // TILE):
-            act(lanes_of(n))
+        loop(EDGES // TILE, lambda n: act(slice(n * TILE, (n + 1) * TILE)))
 
     src = src_ref[...]
     dst = dst_ref[...]
@@ -186,40 +182,33 @@
     live = jnp.where(jnp.logical_and(place < count_ref[...], reach), 1.0, 0.0)
     put_row(LIVE, live)
     slot = jnp.where(ghost, src - ATOMS, src + 8 * GHOST)
-    for j in range(8):
-        lanes = slice(128 * j, 128 * (j + 1))
+    def one_hot(j):
+        lanes = slice(j * 128, (j + 1) * 128)
         oh[0:320, lanes] = (
             lax.broadcasted_iota(jnp.int32, (320, 128), 0) == slot[j : j + 1, :]).astype(F32).astype(BF16)
         hot = (lax.broadcasted_iota(jnp.int32, (ATOMS, 128), 0) == dst[j : j + 1, :]).astype(F32).astype(BF16)
         oh[320:384, lanes] = hot
-        ah[0:64, lanes] = hot
-        al[0:64, lanes] = jnp.zeros((64, 128), BF16)
-
-    back_lhs, back_rhs, fore_lhs, fore_rhs, w0, w0t = [], [], [], [], [], []
-    zero = jnp.zeros((C, C), F32)
-    for layer in range(LAYERS):
-        rows_fl, rows_fr, rows_bl, rows_br = [], [], [], []
-        for d in range(3):
+        ah[512:576, lanes] = hot
+
+    loop(8, one_hot)
+
+    def four(x):
+        hi, lo = split(x)
+        return jnp.concatenate([hi, hi, lo, lo], axis=1)
+
+    def weigh(layer):
+        for i, d in enumerate((1, 2, 0)):
             env_hi, env_lo = split(wv_ref[layer, :, d * C : (d + 1) * C])
-            upd_hi, upd_lo = split(wu_ref[layer, :, (d + 1) * C : (d + 2) * C])
-            m = dot_t(jnp.concatenate([upd_hi, upd_hi, upd_lo, upd_lo], axis=1),
-                      jnp.concatenate([env_hi, env_lo, env_hi, env_lo], axis=1)) * SCALE
-            mt = m.T
-            mh, ml = split(jnp.concatenate([m, m], axis=1))
-            rows_fl.append((jnp.concatenate([mh, ml], axis=0), mh))
-            th, tl = split(jnp.concatenate([mt, mt], axis=1))
-            rows_bl.append((jnp.concatenate([th, tl], axis=0), th))
-            wide = jnp.concatenate([mt, zero], axis=1)
-            rows_fr.append(split(jnp.concatenate([wide, wide], axis=0)))
-            wide = jnp.concatenate([zero, m], axis=1)
-            rows_br.append(split(jnp.concatenate([wide, wide], axis=0)))
-        fore_lhs.append(rows_fl)
-        fore_rhs.append(rows_fr)
-        back_lhs.append(rows_bl)
-        back_rhs.append(rows_br)
+            upd = wu_ref[layer, :, (d + 1) * C : (d + 2) * C] * SCALE
+            m = dot_t(four(upd), jnp.concatenate([env_hi, env_lo, env_hi, env_lo], axis=1))
+            lhs[layer, 64 * i : 64 * (i + 1)] = four(m)
+            lhs[3 - layer, 64 * i : 64 * (i + 1)] = four(m.T)
         own_w = wu_ref[layer, :, 0:C]
-        w0.append(own_w.T)
-        w0t.append(own_w)
+        for stage, x in ((layer, own_w), (3 - layer, own_w.T)):
+            hi, lo = split(x)
+            own_weights[stage] = jnp.concatenate([hi, hi, lo], axis=1)
+
+    loop(LAYERS, weigh)
     wrt = we_ref[:, 2 * C : 2 * C + NB]
     wr = jnp.concatenate([wrt, jnp.zeros((C, 128 - NB), F32)], axis=1).T[0:NB, :]
     wr_low = wr - wr.astype(BF16).astype(F32)
@@ -263,17 +252,18 @@
     put_row(SLOPE, live * slope)
     for i, v in ((UX, ux), (UY, uy), (UZ, uz), (INV, inv)):
         put_row(i, v)
-    for m in range(8):
-        for j in range(8):
-            lanes = slice(128 * j, 128 * (j + 1))
-            wide = jnp.broadcast_to(harm[m][j : j + 1, :], (16, 128))
-            high, low = split(wide)
-            hot = ah[0:64, lanes]
-            ah[64 * (m + 1) : 64 * (m + 2), lanes] = hot * jnp.concatenate([high] * 4, axis=0)
-            al[64 * (m + 1) : 64 * (m + 2), lanes] = hot * jnp.concatenate([low] * 4, axis=0)
+    def map_edges(j):
+        lanes = slice(j * 128, (j + 1) * 128)
+        hot = ah[512:576, lanes]
+        for m in range(8):
+            high, low = split(jnp.broadcast_to(harm[m][j : j + 1, :], (16, 128)))
+            ah[64 * m : 64 * (m + 1), lanes] = hot * jnp.concatenate([high] * 4, axis=0)
+            al[64 * m : 64 * (m + 1), lanes] = hot * jnp.concatenate([low] * 4, axis=0)
+
+    loop(8, map_edges)
 
     emb_hi, emb_lo = split(jnp.concatenate([ghosts[0:C, :], own_src, own_dst], axis=1))
-    emb = jnp.concatenate(
+    embs[...] = jnp.concatenate(
         [jnp.concatenate([emb_hi, wr4], axis=1), jnp.concatenate([emb_lo, jnp.zeros((C, 128), BF16)], axis=1)], axis=0)
     order = (lax.broadcasted_iota(jnp.int32, (NB, TILE), 0) + 1).astype(F32)
 
@@ -282,9 +272,8 @@
         vh[place : place + C, lanes] = hi
         vl[place : place + C, lanes] = lo
         ah[576:640, lanes] = hi
-        al[576:640, lanes] = lo
-        two[0:C, lanes] = hi
-        two[C : 2 * C, lanes] = lo
+        ah[640:704, lanes] = lo
+        ah[704:768, lanes] = hi
 
     def activate(lanes, stage, q):
         s = 1.0 / (1.0 + jnp.exp(-q))
@@ -313,30 +302,37 @@
         dradial_map[:, lanes] = order * (math.pi / CUTOFF) * cosine * near + sine * row[BEND : BEND + 1, lanes]
         low = radial - radial.astype(BF16).astype(F32)
         oh[384:512, lanes] = jnp.concatenate([radial, low, radial, jnp.zeros((104, TILE), F32)], axis=0).astype(BF16)
-        both = dot(emb, oh[:, lanes])
+        both = dot(embs[...], oh[:, lanes])
         f = activate(lanes, 0, both[0:C] + both[C : 2 * C])
         df[:, lanes] = f
         keep(lanes, 192, f)
 
-    def environment():
-        first = dot_t(ah[0:576, :], two[...])
-        return first[0:64], first[64:576] + dot_t(al[64:576, :], two[...])
-
-    def mixed(parts, lhs, rhs, own_w):
-        flat, tall = [], []
-        for d in range(3):
-            lo, hi = SPAN[d]
-            x = split(parts[0] if d == 0 else parts[1][lo - 64 : hi - 64])
-            both = dot_t(lhs[d][0], x[0])
-            flat.append(both[0:C] + both[C : 2 * C] + dot_t(lhs[d][1], x[1]))
-            if d:
-                tall.append(mul3(x, rhs[d]))
-        hi, lo = split(jnp.concatenate(flat + [own_w], axis=1))
-        return (jnp.concatenate([hi, lo], axis=0), hi), jnp.concatenate(tall, axis=0)
-
-    def spread(lanes, flat):
-        both = dot(flat[0], ah[:, lanes])
-        return both[0:C] + both[C : 2 * C] + dot(flat[1], al[:, lanes])
+    degree = lax.broadcasted_iota(jnp.int32, (C, 512), 1) >= 192
+
+    def mix(stage, place):
+        sums = dot_t(ah[576:704, :], ah[0:576, :])
+        sums = sums[0:C] + sums[C : 2 * C]
+        hi, lo = split(sums[:, 0:512] + dot_t(ah[576:640, :], al[...]))
+        every = dot(lhs[stage, 0:128], jnp.concatenate([hi, lo, hi, lo], axis=0))
+        outer = jnp.where(degree, every[C : 2 * C], every[0:C])
+        kept[place : place + C, :] = outer
+        hi, lo = split(sums[:, 512:576])
+        inner = dot(lhs[stage, 128:192], jnp.concatenate([hi, lo, hi, lo], axis=0))
+        hi, lo = split(outer)
+        flat[0:C, 0:512] = hi
+        flat[C : 2 * C, 0:512] = lo
+        hi, lo = split(inner)
+        flat[0:C, 512:768] = jnp.concatenate([hi, own_weights[stage]], axis=1)
+        flat[C : 2 * C, 512:768] = jnp.concatenate([lo, jnp.zeros((C, 192), BF16)], axis=1)
+
+    def spread(lanes):
+        both = dot(flat[...], ah[:, lanes])
+        return both[0:C] + both[C : 2 * C] + dot(flat[0:C, 0:512], al[:, lanes])
+
+    def back_map(place):
+        hi, lo = split(kept[place : place + 128, :].T)
+        uth[:, place : place + 128] = hi
+        utl[:, place : place + 128] = lo
 
     def energy_copy(ph, t):
         me = member(ph)
@@ -366,19 +362,16 @@
     last = len(phases) - 1
 
     tiles(embed)
-    flat, map0 = mixed(environment(), fore_lhs[0], fore_rhs[0], w0t[0])
 
     def first_layer(lanes):
-        f = df[:, lanes] + activate(lanes, 1, spread(lanes, flat))
+        f = df[:, lanes] + activate(lanes, 1, spread(lanes))
         df[:, lanes] = f
         keep(lanes, 64, f)
 
-    tiles(first_layer)
-    flat, map1 = mixed(environment(), fore_lhs[1], fore_rhs[1], w0t[1])
-    pieces = []
+    folded[...] = jnp.zeros((8, TILE), F32)
 
     def turn(lanes):
-        q = spread(lanes, flat)
+        q = spread(lanes)
         s = 1.0 / (1.0 + jnp.exp(-q))
         v = q * s
         cut = row[CUT : CUT + 1, lanes]
@@ -388,40 +381,41 @@
         piece = per_edge[0:8]
         for i in range(1, 8):
             piece = piece + per_edge[8 * i : 8 * i + 8]
-        pieces.append(piece[:, 0:128] + piece[:, 128:256])
+        folded[...] += piece
         df[:, lanes] = g
         row[DCUT : DCUT + 1, lanes] = jnp.sum(g * v, axis=0, keepdims=True)
         keep(lanes, 0, g * ((s + v * (1.0 - s)) * cut))
 
-    tiles(turn)
-    energy_out(0, (pieces[0] + pieces[1]) + (pieces[2] + pieces[3]))
-
-    flat, tall = mixed(environment(), back_lhs[1], back_rhs[1], w0[1])
-    ut1 = map1 + tall
-
     def back_first(lanes):
-        g = df[:, lanes] + spread(lanes, flat)
+        g = df[:, lanes] + spread(lanes)
         df[:, lanes] = g
         row[DCUT : DCUT + 1, lanes] += jnp.sum(g * value[1, :, lanes], axis=0, keepdims=True)
         keep(lanes, 128, g * gain_cut[1, :, lanes])
 
+    mix(0, 128)
+    tiles(first_layer)
+    mix(1, 0)
+    tiles(turn)
+    energy_out(0, folded[:, 0:128] + folded[:, 128:256])
+    mix(2, 64)
     tiles(back_first)
     for ph in range(0, min(1, last)):
         energy_out(ph + 1, energy_in(ph))
-    flat, tall = mixed(environment(), back_lhs[0], back_rhs[0], w0[0])
+    back_map(0)
+    mix(3, 192)
     for ph in range(1, min(2, last)):
         energy_out(ph + 1, energy_in(ph))
-    uh, ul = split(jnp.concatenate([ut1, map0 + tall], axis=1))
+    back_map(128)
 
     def back_embed(lanes):
-        g = df[:, lanes] + spread(lanes, flat)
+        g = df[:, lanes] + spread(lanes)
         dcut = row[DCUT : DCUT + 1, lanes] + jnp.sum(g * value[0, :, lanes], axis=0, keepdims=True)
         both = dot(wr2, jnp.concatenate(split(g * gain_cut[0, :, lanes]), axis=0))
         dr = jnp.sum((both[0:8] + both[8:16]) * dradial_map[:, lanes], axis=0, keepdims=True)
         dr = dr + dcut * row[SLOPE : SLOPE + 1, lanes]
         right = vh[:, lanes]
-        part = dot(uh, right) + dot(ul, right) + dot(uh, vl[:, lanes])
-        hot = ah[0:64, lanes].astype(F32)
+        part = dot(uth[...], right) + dot(utl[...], right) + dot(uth[...], vl[:, lanes])
+        hot = ah[512:576, lanes].astype(F32)
         g = [jnp.sum(hot * part[64 * m : 64 * (m + 1)], axis=0, keepdims=True) for m in range(8)]
         xr, yr, zr, ir = (row[i : i + 1, lanes] for i in (UX, UY, UZ, INV))
         dux = g[0] + root * (g[3] * yr + g[6] * zr + g[7] * xr)
@@ -498,18 +492,25 @@
                 pltpu.VMEM((1, C), F32),
                 pltpu.VMEM((GHOST, 128), F32),
                 pltpu.VMEM((8, GHOST, 128), F32),
-                pltpu.VMEM((640, EDGES), BF16),
-                pltpu.VMEM((640, EDGES), BF16),
+                pltpu.VMEM((768, EDGES), BF16),
+                pltpu.VMEM((512, EDGES), BF16),
                 pltpu.VMEM((512, EDGES), BF16),
                 pltpu.VMEM((256, EDGES), BF16),
                 pltpu.VMEM((256, EDGES), BF16),
-                pltpu.VMEM((128, EDGES), BF16),
                 pltpu.VMEM((16, EDGES), F32),
                 pltpu.VMEM((2, C, EDGES), F32),
                 pltpu.VMEM((2, C, EDGES), F32),
                 pltpu.VMEM((C, EDGES), F32),
                 pltpu.VMEM((NB, EDGES), F32),
                 pltpu.VMEM((16, EDGES), BF16),
+                pltpu.VMEM((2 * LAYERS, 192, 256), BF16),
+                pltpu.VMEM((2 * LAYERS, C, 192), BF16),
+                pltpu.VMEM((128, 768), BF16),
+                pltpu.VMEM((256, 512), F32),
+                pltpu.VMEM((8, TILE), F32),
+                pltpu.VMEM((512, 256), BF16),
+                pltpu.VMEM((512, 256), BF16),
+                pltpu.VMEM((128, 512), BF16),
                 pltpu.VMEM((2, 8, 128), F32),
                 pltpu.VMEM((8, 8, 128), F32),
                 pltpu.VMEM((len(phases), most, 8, 128), F32),

time: 44.8 us -> 43.4 us (0.969)
  Pallas kernels: 40.4 us -> 39 us
    pallas_call x1, Pallas kernels: 40.4 us -> 39 us  [per_device(): pl.pallas_call(body, out_shape=(jax.ShapeDtypeStruct((3, ATOMS), F32), ja...]
where the time goes in v2:
time: 43.4 us; the launch traced here: 43.2 us
  Pallas kernels  39 us (90%)
  between operations  3.06 us (7%)
  local copies, waits for them, and re-layouts  1.22 us (3%)
    pallas_call x1, Pallas kernels, per_device(): pl.pallas_call(body, out_shape=(jax.ShapeDtypeStruct((3, ATOMS), F32), ja...  39 us
    unnamed x3, local copies, waits for them, and re-layouts  1.22 us

profile of v2, /device:TPU:1, one launch (start us, length us, event | category | flops | bytes accessed | tf_op | source)
XLA Modules:
  0.0 43.2 jit_solution(610564557661171586)
XLA Ops:
  1.3 39.0 %shard_map.113 = (f32[3,64]{1,0:T(4,128)}, f32[1,1]{1,0:T(1,128)}) custom-call(f32[3,64]{1,0:T(4,128)} %refs_0_.1, bf16[64,64]{1,0:T(8,128)(2,1)} %refs_1_.1, s32[1,32]{1,0:T(1,128)} %bitcast.13, s32[8,128]{1,0:T(8,128)} %bitcast.11, s32[8,128]{1,0:T(8,128)} %bitcast.12, s32[1,1]{1,0:T(1,128)} %bitcast.8.refs_5_, f32[64,136]{1,0:T(8,128)} %bitcast.10, ...), custom_call_target="tpu_custom_call" | custom-call | tf_op jit(solution)/shard_map/pallas_call | solution.py:477
  40.2 0.0 copy-start
  40.2 0.6 %copy-done = f32[3,64]{1,0:T(4,128)S(1)} copy-done((f32[3,64]{1,0:T(4,128)S(1)}, f32[3,64]{1,0:T(4,128)}, u32[]{:S(2)}) %copy-start) | copy-done | bytes 792
  40.9 0.6 %copy.15 = f32[3,64]{1,0:T(4,128)} copy(f32[3,64]{1,0:T(4,128)S(1)} %copy-done) | data formatting | bytes 1536
Async XLA Ops:
  40.2 0.7 %copy-start = (f32[3,64]{1,0:T(4,128)S(1)}, f32[3,64]{1,0:T(4,128)}, u32[]{:S(2)}) copy-start(f32[3,64]{1,0:T(4,128)} %get-tuple-element.8) | copy-start | bytes 2308

commit v3 on v2

--- a/solution.py
+++ b/solution.py
@@ -55,19 +55,12 @@
     return result
 
 
-def phases_of(columns, rows):
-    phases = []
-    stride = 1
-    while stride < columns:
-        size = 4 if (columns // stride) % 4 == 0 else columns // stride
-        phases.append(("gx", stride, size))
-        stride *= size
-    phases.append(("gy", 1, rows))
-    return phases
+def sizes_of(columns, rows):
+    return (4 * rows, columns // 4)
 
 
 def kernel(
-    columns, rows, phases,
+    columns, rows, sizes,
     pos_in, feat_in, send_in, src_in, dst_in, count_in, we_in, wv_in, wu_in, wo_in,
     forces_ref, energy_ref,
     pos_ref, feat_ref, send_ref, src_ref, dst_ref, count_ref, we_ref, wv_ref, wu_ref, wo_ref,
@@ -93,22 +86,20 @@
             pl.when(jnp.logical_not(good))(otherwise)
 
     def member(ph):
-        axis, stride, size = phases[ph]
-        index = a if axis == "gx" else b
-        return lax.rem(index // stride, size)
+        return lax.rem(a, 4) * rows + b if ph == 0 else a // 4
 
     def energy_peer(ph, t):
-        axis, stride, size = phases[ph]
-        me = member(ph)
-        step = (lax.rem(me + t, size) - me) * stride
-        return (a + step, b) if axis == "gx" else (a, b + step)
+        other = lax.rem(member(ph) + t, sizes[ph])
+        if ph == 0:
+            return (a - lax.rem(a, 4) + other // rows, lax.rem(other, rows))
+        return (lax.rem(a, 4) + 4 * other, b)
 
     barrier = pltpu.get_barrier_semaphore()
     for k in range(8):
         when_valid(k, lambda k=k: pl.semaphore_signal(barrier, inc=1, device_id=peer(k), device_id_type=MESH))
     greeted = 0
-    for ph in range(len(phases)):
-        for t in range(1, phases[ph][2]):
+    for ph in range(2):
+        for t in range(1, sizes[ph]):
             pl.semaphore_signal(barrier, inc=1, device_id=energy_peer(ph, t), device_id_type=MESH)
             greeted += 1
 
@@ -343,11 +334,11 @@
 
     def energy_out(ph, x):
         ebuf[ph, member(ph)] = x
-        for t in range(1, phases[ph][2]):
+        for t in range(1, sizes[ph]):
             energy_copy(ph, t).start()
 
     def energy_in(ph):
-        size = phases[ph][2]
+        size = sizes[ph]
         for t in range(1, size):
             came = lax.rem(member(ph) + size - t, size)
             pltpu.make_async_remote_copy(
@@ -358,8 +349,6 @@
         for t in range(1, size):
             total = total + ebuf[ph, t]
         return total
-
-    last = len(phases) - 1
 
     tiles(embed)
 
@@ -399,13 +388,10 @@
     energy_out(0, folded[:, 0:128] + folded[:, 128:256])
     mix(2, 64)
     tiles(back_first)
-    for ph in range(0, min(1, last)):
-        energy_out(ph + 1, energy_in(ph))
     back_map(0)
     mix(3, 192)
-    for ph in range(1, min(2, last)):
-        energy_out(ph + 1, energy_in(ph))
     back_map(128)
+    energy_out(1, energy_in(0))
 
     def back_embed(lanes):
         g = df[:, lanes] + spread(lanes)
@@ -427,8 +413,6 @@
         ddb[:, lanes] = jnp.concatenate([dd, dd - dd.astype(BF16).astype(F32)], axis=0).astype(BF16)
 
     tiles(back_embed)
-    for ph in range(2, last):
-        energy_out(ph + 1, energy_in(ph))
     scattered = dot_t(ddb[...], oh[0:384, :])
     scattered = scattered[0:8] + scattered[8:16]
     gsrc[0] = scattered[:, 0:128]
@@ -451,32 +435,32 @@
     acc_low = acc - acc.astype(BF16).astype(F32)
     returned = dot_t(jnp.concatenate([acc, acc_low], axis=0).astype(BF16), st4)
     returned = returned[0:8] + returned[8:16]
-    forces_ref[...] = -(at_own + returned)[0:3, :]
-
-    total = energy_in(last)
+    forces_ref[...] = -(at_own + returned)
+
+    total = energy_in(1)
     energy_ref[...] = jnp.sum(jnp.sum(total, axis=0, keepdims=True), axis=1, keepdims=True)
 
     for k in range(8):
         when_valid(k, lambda k=k: (ghost_copy(k).wait_send(), force_copy(k).wait_send())[0])
-    for ph in range(len(phases)):
-        for t in range(1, phases[ph][2]):
+    for ph in range(2):
+        for t in range(1, sizes[ph]):
             energy_copy(ph, t).wait_send()
 
 
 def solution(mesh):
     columns, rows = mesh.shape["gx"], mesh.shape["gy"]
-    phases = phases_of(columns, rows)
-    most = max(size for _, _, size in phases)
+    sizes = sizes_of(columns, rows)
+    most = max(sizes)
 
     def per_device(positions, features, send_list, edge_src, edge_dst, edge_count, w_embed, w_env, w_update, w_out):
         def body(*refs):
-            kernel(columns, rows, phases, *refs)
+            kernel(columns, rows, sizes, *refs)
 
         vmem = pl.BlockSpec(memory_space=pltpu.VMEM)
         anywhere = pl.BlockSpec(memory_space=pl.ANY)
         forces, energy = pl.pallas_call(
             body,
-            out_shape=(jax.ShapeDtypeStruct((3, ATOMS), F32), jax.ShapeDtypeStruct((1, 1), F32)),
+            out_shape=(jax.ShapeDtypeStruct((8, ATOMS), F32), jax.ShapeDtypeStruct((1, 1), F32)),
             in_specs=[anywhere] * 10,
             out_specs=(vmem, vmem),
             scratch_shapes=[
@@ -513,14 +497,14 @@
                 pltpu.VMEM((128, 512), BF16),
                 pltpu.VMEM((2, 8, 128), F32),
                 pltpu.VMEM((8, 8, 128), F32),
-                pltpu.VMEM((len(phases), most, 8, 128), F32),
+                pltpu.VMEM((2, most, 8, 128), F32),
                 pltpu.SemaphoreType.DMA((10,)),
                 pltpu.SemaphoreType.DMA((8,)),
                 pltpu.SemaphoreType.DMA((8,)),
                 pltpu.SemaphoreType.DMA((8,)),
                 pltpu.SemaphoreType.DMA((8,)),
-                pltpu.SemaphoreType.DMA((len(phases), most)),
-                pltpu.SemaphoreType.DMA((len(phases), most)),
+                pltpu.SemaphoreType.DMA((2, most)),
+                pltpu.SemaphoreType.DMA((2, most)),
             ],
             compiler_params=pltpu.CompilerParams(
                 collective_id=0, has_side_effects=True, vmem_limit_bytes=60 * 1024 * 1024
@@ -529,7 +513,7 @@
             positions, features, send_list.reshape(1, GHOST), edge_src.reshape(8, 128), edge_dst.reshape(8, 128),
             edge_count.reshape(1, 1), w_embed.T, w_env, jnp.swapaxes(w_update, 1, 2), w_out.reshape(1, C),
         )
-        return forces, energy.reshape(())
+        return forces[0:3], energy.reshape(())
 
     placed = (
         P(None, ("gx", "gy")), P(None, ("gx", "gy")), P(("gx", "gy")), P(("gx", "gy")), P(("gx", "gy")),

time: 43.4 us -> 41.5 us (0.956)
  Pallas kernels: 39 us -> 37 us
    pallas_call x1, Pallas kernels: 39 us -> 37 us  [per_device(): pl.pallas_call(body, out_shape=(jax.ShapeDtypeStruct((8, ATOMS), F32), ja...]
    slice x0 -> x1, local copies, waits for them, and re-layouts: none -> 0.58 us  [per_device(): return (forces[0:3], energy.reshape(()))]
    unnamed x3 -> x2, local copies, waits for them, and re-layouts: 1.22 us -> 0.66 us
where the time goes in v3:
time: 41.5 us; the launch traced here: 41.3 us
  Pallas kernels  37 us (89%)
  between operations  3.06 us (7%)
  local copies, waits for them, and re-layouts  1.24 us (3%)
    pallas_call x1, Pallas kernels, per_device(): pl.pallas_call(body, out_shape=(jax.ShapeDtypeStruct((8, ATOMS), F32), ja...  37 us

profile of v3, /device:TPU:1, one launch (start us, length us, event | category | flops | bytes accessed | tf_op | source)
XLA Modules:
  0.0 41.3 jit_solution(6402503849648977417)
XLA Ops:
  1.3 37.0 %shard_map.113 = (f32[8,64]{1,0:T(8,128)}, f32[1,1]{1,0:T(1,128)}) custom-call(f32[3,64]{1,0:T(4,128)} %refs_0_.1, bf16[64,64]{1,0:T(8,128)(2,1)} %refs_1_.1, s32[1,32]{1,0:T(1,128)} %bitcast.13, s32[8,128]{1,0:T(8,128)} %bitcast.11, s32[8,128]{1,0:T(8,128)} %bitcast.12, s32[1,1]{1,0:T(1,128)} %bitcast.8.refs_5_, f32[64,136]{1,0:T(8,128)} %bitcast.10, ...), custom_call_target="tpu_custom_call" | custom-call | tf_op jit(solution)/shard_map/pallas_call | solution.py:461
  38.3 0.0 copy-start
  38.3 0.7 %copy-done = f32[8,64]{1,0:T(8,128)S(1)} copy-done((f32[8,64]{1,0:T(8,128)S(1)}, f32[8,64]{1,0:T(8,128)}, u32[]{:S(2)}) %copy-start) | copy-done | bytes 2072
  39.0 0.6 %slice.3 = f32[3,64]{1,0:T(4,128)} slice(f32[8,64]{1,0:T(8,128)S(1)} %copy-done), slice={[0:3], [0:64]} | slice | bytes 1536 | tf_op jit(solution)/shard_map/slice | solution.py:516
Async XLA Ops:
  38.3 0.7 %copy-start = (f32[8,64]{1,0:T(8,128)S(1)}, f32[8,64]{1,0:T(8,128)}, u32[]{:S(2)}) copy-start(f32[8,64]{1,0:T(8,128)} %get-tuple-element.4) | copy-start | bytes 6148

commit v4 on v3

--- a/solution.py
+++ b/solution.py
@@ -15,6 +15,9 @@
 EDGES = 1024
 SCALE = 16 ** (-0.5)
 OFFSETS = ((-1, -1), (-1, 0), (-1, 1), (0, -1), (0, 1), (1, -1), (1, 0), (1, 1))
+GROUPS = ((0, 3, 5), (1, 6), (2, 4, 7))
+SPANS = ((0, 3), (3, 5), (5, 8))
+PLACE = (0, 3, 5, 1, 6, 2, 4, 7)
 WIDTH = 6.0
 CUTOFF = 5.0
 F32 = jnp.float32
@@ -56,13 +59,13 @@
 
 
 def sizes_of(columns, rows):
-    return (4 * rows, columns // 4)
+    return (2 * rows, max(columns // 8, 1), min(4, columns // 2))
 
 
 def kernel(
     columns, rows, sizes,
     pos_in, feat_in, send_in, src_in, dst_in, count_in, we_in, wv_in, wu_in, wo_in,
-    forces_ref, energy_ref,
+    out_ref,
     pos_ref, feat_ref, send_ref, src_ref, dst_ref, count_ref, we_ref, wv_ref, wu_ref, wo_ref,
     pay, table, ah, al, oh, vh, vl, row, value, gain_cut, df, dradial_map, ddb, lhs, own_weights, flat, kept, folded,
     uth, utl, embs, gsrc, gbuf, ebuf,
@@ -75,30 +78,37 @@
         dx, dy = OFFSETS[k]
         return (lax.rem(a + dx + columns, columns), b + dy)
 
-    def when_valid(k, act, otherwise=None):
-        dy = OFFSETS[k][1]
-        if dy == 0:
-            act()
-            return
-        good = (b > 0) if dy < 0 else (b < rows - 1)
-        pl.when(good)(act)
-        if otherwise is not None:
-            pl.when(jnp.logical_not(good))(otherwise)
+    def group_of(k):
+        return 1 + OFFSETS[k][1]
+
+    def each_group(act, otherwise=None):
+        act(1)
+        for g, good in ((0, b > 0), (2, b < rows - 1)):
+            pl.when(good)(lambda g=g: act(g))
+            if otherwise is not None:
+                pl.when(jnp.logical_not(good))(lambda g=g: otherwise(g))
 
     def member(ph):
-        return lax.rem(a, 4) * rows + b if ph == 0 else a // 4
+        if ph == 0:
+            return lax.rem(a, 2) * rows + b
+        return a // 8 if ph == 1 else lax.rem(a // 2, sizes[2])
 
     def energy_peer(ph, t):
-        other = lax.rem(member(ph) + t, sizes[ph])
+        me = member(ph)
+        other = lax.rem(me + t, sizes[ph])
         if ph == 0:
-            return (a - lax.rem(a, 4) + other // rows, lax.rem(other, rows))
-        return (lax.rem(a, 4) + 4 * other, b)
+            return (a - lax.rem(a, 2) + other // rows, lax.rem(other, rows))
+        return (a + (8 if ph == 1 else 2) * (other - me), b)
 
     barrier = pltpu.get_barrier_semaphore()
-    for k in range(8):
-        when_valid(k, lambda k=k: pl.semaphore_signal(barrier, inc=1, device_id=peer(k), device_id_type=MESH))
+
+    def greet(g):
+        for k in GROUPS[g]:
+            pl.semaphore_signal(barrier, inc=1, device_id=peer(k), device_id_type=MESH)
+
+    each_group(greet)
     greeted = 0
-    for ph in range(2):
+    for ph in range(3):
         for t in range(1, sizes[ph]):
             pl.semaphore_signal(barrier, inc=1, device_id=energy_peer(ph, t), device_id_type=MESH)
             greeted += 1
@@ -135,12 +145,23 @@
 
     def ghost_copy(k):
         return pltpu.make_async_remote_copy(
-            src_ref=pay, dst_ref=table.at[7 - k], send_sem=send_sem.at[k], recv_sem=recv_sem.at[7 - k],
-            device_id=peer(k), device_id_type=MESH,
+            src_ref=pay, dst_ref=table.at[PLACE[7 - k]], send_sem=send_sem.at[group_of(k)],
+            recv_sem=recv_sem.at[group_of(7 - k)], device_id=peer(k), device_id_type=MESH,
         )
 
-    for k in range(8):
-        when_valid(k, lambda k=k: ghost_copy(k).start())
+    def ghost_group(g):
+        held = table.at[pl.ds(SPANS[g][0], len(GROUPS[g]))]
+        return pltpu.make_async_remote_copy(
+            src_ref=held, dst_ref=held, send_sem=send_sem.at[g], recv_sem=recv_sem.at[g],
+            device_id=peer(GROUPS[g][0]), device_id_type=MESH,
+        )
+
+    def ghosts_out(g):
+        for k in GROUPS[g]:
+            ghost_copy(k).start()
+
+    each_group(ghosts_out)
+
     for copy in fetched[4:]:
         copy.wait()
 
@@ -161,18 +182,20 @@
     ghost = src >= ATOMS
     ox = jnp.zeros((8, 128), F32)
     oy = jnp.zeros((8, 128), F32)
+    block_place = jnp.zeros((8, 128), jnp.int32)
     for k, (dx, dy) in enumerate(OFFSETS):
         here = jnp.logical_and(ghost, block == k)
         if dx:
             ox = jnp.where(here, WIDTH * dx, ox)
         if dy:
             oy = jnp.where(here, WIDTH * dy, oy)
+        block_place = jnp.where(here, PLACE[k], block_place)
     step_y = (oy * (1.0 / WIDTH)).astype(jnp.int32)
     reach = jnp.logical_and(b + step_y >= 0, b + step_y < rows)
     place = lax.broadcasted_iota(jnp.int32, (8, 128), 0) * 128 + lax.broadcasted_iota(jnp.int32, (8, 128), 1)
     live = jnp.where(jnp.logical_and(place < count_ref[...], reach), 1.0, 0.0)
     put_row(LIVE, live)
-    slot = jnp.where(ghost, src - ATOMS, src + 8 * GHOST)
+    slot = jnp.where(ghost, block_place * GHOST + (src & (GHOST - 1)), src + 8 * GHOST)
     def one_hot(j):
         lanes = slice(j * 128, (j + 1) * 128)
         oh[0:320, lanes] = (
@@ -187,19 +210,21 @@
         hi, lo = split(x)
         return jnp.concatenate([hi, hi, lo, lo], axis=1)
 
-    def weigh(layer):
+    def weigh(stage):
+        layer = min(stage, 3 - stage)
         for i, d in enumerate((1, 2, 0)):
             env_hi, env_lo = split(wv_ref[layer, :, d * C : (d + 1) * C])
-            upd = wu_ref[layer, :, (d + 1) * C : (d + 2) * C] * SCALE
-            m = dot_t(four(upd), jnp.concatenate([env_hi, env_lo, env_hi, env_lo], axis=1))
-            lhs[layer, 64 * i : 64 * (i + 1)] = four(m)
-            lhs[3 - layer, 64 * i : 64 * (i + 1)] = four(m.T)
+            upd_hi, upd_lo = split(wu_ref[layer, :, (d + 1) * C : (d + 2) * C] * SCALE)
+            env = [env_hi, env_lo, env_hi, env_lo]
+            upd = [upd_hi, upd_hi, upd_lo, upd_lo]
+            left, right = (upd, env) if stage < LAYERS else (env, upd)
+            lhs[stage, 64 * i : 64 * (i + 1)] = four(
+                dot_t(jnp.concatenate(left, axis=1), jnp.concatenate(right, axis=1)))
         own_w = wu_ref[layer, :, 0:C]
-        for stage, x in ((layer, own_w), (3 - layer, own_w.T)):
-            hi, lo = split(x)
-            own_weights[stage] = jnp.concatenate([hi, hi, lo], axis=1)
-
-    loop(LAYERS, weigh)
+        hi, lo = split(own_w if stage < LAYERS else own_w.T)
+        own_weights[stage] = jnp.concatenate([hi, hi, lo], axis=1)
+
+    weigh(0)
     wrt = we_ref[:, 2 * C : 2 * C + NB]
     wr = jnp.concatenate([wrt, jnp.zeros((C, 128 - NB), F32)], axis=1).T[0:NB, :]
     wr_low = wr - wr.astype(BF16).astype(F32)
@@ -209,12 +234,12 @@
     diagonal = lax.broadcasted_iota(jnp.int32, (C, C), 0) == lax.broadcasted_iota(jnp.int32, (C, C), 1)
     wo = jnp.sum(jnp.where(diagonal, wo_ref[...], 0.0), axis=1, keepdims=True)
 
-    def blank(k):
-        table[k] = jnp.zeros((GHOST, 128), F32)
-        gbuf[k] = jnp.zeros((8, 128), F32)
-
-    for k in range(8):
-        when_valid(k, lambda k=k: ghost_copy(7 - k).wait_recv(), lambda k=k: blank(k))
+    def blank(g):
+        for i in range(*SPANS[g]):
+            table[i] = jnp.zeros((GHOST, 128), F32)
+            gbuf[i] = jnp.zeros((8, 128), F32)
+
+    each_group(lambda g: ghost_group(g).wait_recv(), blank)
 
     ghosts = jnp.concatenate([table[0:4].reshape(128, 128).T, table[4:8].reshape(128, 128).T], axis=1)
     own_pos = jnp.concatenate([pos, jnp.zeros((3, 64), F32)], axis=1)
@@ -325,31 +350,31 @@
         uth[:, place : place + 128] = hi
         utl[:, place : place + 128] = lo
 
-    def energy_copy(ph, t):
+    def energy_out(ph, x):
         me = member(ph)
+        ebuf[ph, me] = x
+        for t in range(1, sizes[ph]):
+            pltpu.make_async_remote_copy(
+                src_ref=ebuf.at[ph, me], dst_ref=ebuf.at[ph, me], send_sem=esend_sem.at[ph], recv_sem=erecv_sem.at[ph],
+                device_id=energy_peer(ph, t), device_id_type=MESH,
+            ).start()
+
+    def energy_group(ph):
+        held = ebuf.at[ph, pl.ds(0, sizes[ph] - 1)]
         return pltpu.make_async_remote_copy(
-            src_ref=ebuf.at[ph, me], dst_ref=ebuf.at[ph, me], send_sem=esend_sem.at[ph, t],
-            recv_sem=erecv_sem.at[ph, t], device_id=energy_peer(ph, t), device_id_type=MESH,
+            src_ref=held, dst_ref=held, send_sem=esend_sem.at[ph], recv_sem=erecv_sem.at[ph],
+            device_id=energy_peer(ph, 1), device_id_type=MESH,
         )
 
-    def energy_out(ph, x):
-        ebuf[ph, member(ph)] = x
+    def energy_in(ph):
+        if sizes[ph] > 1:
+            energy_group(ph).wait_recv()
+        total = ebuf[ph, 0]
         for t in range(1, sizes[ph]):
-            energy_copy(ph, t).start()
-
-    def energy_in(ph):
-        size = sizes[ph]
-        for t in range(1, size):
-            came = lax.rem(member(ph) + size - t, size)
-            pltpu.make_async_remote_copy(
-                src_ref=ebuf.at[ph, came], dst_ref=ebuf.at[ph, came], send_sem=esend_sem.at[ph, t],
-                recv_sem=erecv_sem.at[ph, t], device_id=energy_peer(ph, t), device_id_type=MESH,
-            ).wait_recv()
-        total = ebuf[ph, 0]
-        for t in range(1, size):
             total = total + ebuf[ph, t]
         return total
 
+    weigh(1)
     tiles(embed)
 
     def first_layer(lanes):
@@ -382,8 +407,10 @@
         keep(lanes, 128, g * gain_cut[1, :, lanes])
 
     mix(0, 128)
+    weigh(2)
     tiles(first_layer)
     mix(1, 0)
+    weigh(3)
     tiles(turn)
     energy_out(0, folded[:, 0:128] + folded[:, 128:256])
     mix(2, 64)
@@ -419,32 +446,46 @@
     gsrc[1] = scattered[:, 128:256]
     def force_copy(k):
         return pltpu.make_async_remote_copy(
-            src_ref=gsrc.at[k // 4], dst_ref=gbuf.at[7 - k], send_sem=gsend_sem.at[k], recv_sem=grecv_sem.at[7 - k],
-            device_id=peer(k), device_id_type=MESH,
+            src_ref=gsrc.at[PLACE[k] // 4], dst_ref=gbuf.at[PLACE[7 - k]], send_sem=gsend_sem.at[group_of(k)],
+            recv_sem=grecv_sem.at[group_of(7 - k)], device_id=peer(k), device_id_type=MESH,
         )
 
-    for k in range(8):
-        when_valid(k, lambda k=k: force_copy(k).start())
+    def force_group(g):
+        held = gbuf.at[pl.ds(SPANS[g][0], len(GROUPS[g]))]
+        return pltpu.make_async_remote_copy(
+            src_ref=held, dst_ref=held, send_sem=gsend_sem.at[g], recv_sem=grecv_sem.at[g],
+            device_id=peer(GROUPS[g][0]), device_id_type=MESH,
+        )
+
+    def forces_out(g):
+        for k in GROUPS[g]:
+            force_copy(k).start()
+
+    each_group(forces_out)
+    energy_out(2, energy_in(1))
     at_own = scattered[:, 256:320] - scattered[:, 320:384]
-    for k in range(8):
-        when_valid(k, lambda k=k: force_copy(7 - k).wait_recv())
-    group = lax.broadcasted_iota(jnp.int32, (8, 128), 1) >> 5
+    for ph in range(2):
+        if sizes[ph] > 1:
+            energy_group(ph).wait_send()
+    each_group(lambda g: ghost_group(g).wait_send())
+
+    def forces_in(g):
+        force_group(g).wait_recv()
+        force_group(g).wait_send()
+
+    each_group(forces_in)
+    lane_group = lax.broadcasted_iota(jnp.int32, (8, 128), 1) >> 5
     acc = jnp.zeros((8, 128), F32)
     for k in range(8):
-        acc = acc + jnp.where(group == (7 - k) % 4, gbuf[k], 0.0)
+        acc = acc + jnp.where(lane_group == PLACE[7 - k] % 4, gbuf[PLACE[k]], 0.0)
     acc_low = acc - acc.astype(BF16).astype(F32)
     returned = dot_t(jnp.concatenate([acc, acc_low], axis=0).astype(BF16), st4)
-    returned = returned[0:8] + returned[8:16]
-    forces_ref[...] = -(at_own + returned)
-
-    total = energy_in(1)
-    energy_ref[...] = jnp.sum(jnp.sum(total, axis=0, keepdims=True), axis=1, keepdims=True)
-
-    for k in range(8):
-        when_valid(k, lambda k=k: (ghost_copy(k).wait_send(), force_copy(k).wait_send())[0])
-    for ph in range(2):
-        for t in range(1, sizes[ph]):
-            energy_copy(ph, t).wait_send()
+    forces = -(at_own + returned[0:8] + returned[8:16])
+
+    total = energy_in(2)
+    energy = jnp.sum(jnp.sum(total, axis=0, keepdims=True), axis=1, keepdims=True)
+    out_ref[...] = jnp.where(lax.broadcasted_iota(jnp.int32, (8, ATOMS), 0) == 3, energy, forces)
+    energy_group(2).wait_send()
 
 
 def solution(mesh):
@@ -458,11 +499,11 @@
 
         vmem = pl.BlockSpec(memory_space=pltpu.VMEM)
         anywhere = pl.BlockSpec(memory_space=pl.ANY)
-        forces, energy = pl.pallas_call(
+        out = pl.pallas_call(
             body,
-            out_shape=(jax.ShapeDtypeStruct((8, ATOMS), F32), jax.ShapeDtypeStruct((1, 1), F32)),
+            out_shape=jax.ShapeDtypeStruct((8, ATOMS), F32),
             in_specs=[anywhere] * 10,
-            out_specs=(vmem, vmem),
+            out_specs=vmem,
             scratch_shapes=[
                 pltpu.VMEM((3, ATOMS), F32),
                 pltpu.VMEM((C, ATOMS), BF16),
@@ -497,14 +538,14 @@
                 pltpu.VMEM((128, 512), BF16),
                 pltpu.VMEM((2, 8, 128), F32),
                 pltpu.VMEM((8, 8, 128), F32),
-                pltpu.VMEM((2, most, 8, 128), F32),
+                pltpu.VMEM((3, most, 8, 128), F32),
                 pltpu.SemaphoreType.DMA((10,)),
-                pltpu.SemaphoreType.DMA((8,)),
-                pltpu.SemaphoreType.DMA((8,)),
-                pltpu.SemaphoreType.DMA((8,)),
-                pltpu.SemaphoreType.DMA((8,)),
-                pltpu.SemaphoreType.DMA((2, most)),
-                pltpu.SemaphoreType.DMA((2, most)),
+                pltpu.SemaphoreType.DMA((3,)),
+                pltpu.SemaphoreType.DMA((3,)),
+                pltpu.SemaphoreType.DMA((3,)),
+                pltpu.SemaphoreType.DMA((3,)),
+                pltpu.SemaphoreType.DMA((3,)),
+                pltpu.SemaphoreType.DMA((3,)),
             ],
             compiler_params=pltpu.CompilerParams(
                 collective_id=0, has_side_effects=True, vmem_limit_bytes=60 * 1024 * 1024
@@ -513,7 +554,7 @@
             positions, features, send_list.reshape(1, GHOST), edge_src.reshape(8, 128), edge_dst.reshape(8, 128),
             edge_count.reshape(1, 1), w_embed.T, w_env, jnp.swapaxes(w_update, 1, 2), w_out.reshape(1, C),
         )
-        return forces[0:3], energy.reshape(())
+        return out[0:3], out[3, 0]
 
     placed = (
         P(None, ("gx", "gy")), P(None, ("gx", "gy")), P(("gx", "gy")), P(("gx", "gy")), P(("gx", "gy")),

time: 41.5 us -> 39 us (0.940)
  Pallas kernels: 37 us -> 35.1 us
  between operations: 3.06 us -> 1.29 us
  local copies, waits for them, and re-layouts: 1.24 us -> 2.45 us
    pallas_call x1, Pallas kernels: 37 us -> 35.1 us  [per_device(): pl.pallas_call(body, out_shape=jax.ShapeDtypeStruct((8, ATOMS), F32), in_...]
    slice x1 -> x2, local copies, waits for them, and re-layouts: 0.58 us -> 2.45 us  [per_device(): return (out[0:3], out[3, 0])]
    unnamed x2 -> x0, local copies, waits for them, and re-layouts: 0.66 us -> none
where the time goes in v4:
time: 39 us; the launch traced here: 38.8 us
  Pallas kernels  35.1 us (90%)
  local copies, waits for them, and re-layouts  2.45 us (6%)
  between operations  1.29 us (3%)
    pallas_call x1, Pallas kernels, per_device(): pl.pallas_call(body, out_shape=jax.ShapeDtypeStruct((8, ATOMS), F32), in_...  35.1 us
    slice x2, local copies, waits for them, and re-layouts, per_device(): return (out[0:3], out[3, 0])  2.45 us

profile of v4, /device:TPU:1, one launch (start us, length us, event | category | flops | bytes accessed | tf_op | source)
XLA Modules:
  0.0 38.8 jit_solution(16837886774023314897)
XLA Ops:
  1.3 35.1 %shard_map.113 = f32[8,64]{1,0:T(8,128)} custom-call(f32[3,64]{1,0:T(4,128)} %refs_0_.1, bf16[64,64]{1,0:T(8,128)(2,1)} %refs_1_.1, s32[1,32]{1,0:T(1,128)} %bitcast.13, s32[8,128]{1,0:T(8,128)} %bitcast.11, s32[8,128]{1,0:T(8,128)} %bitcast.12, s32[1,1]{1,0:T(1,128)} %bitcast.8.refs_5_, f32[64,136]{1,0:T(8,128)} %bitcast.10, f32[2,64,192]{2,1,0:T(8,128)} %refs_7_.1, ...), custom_call_target="tpu_custom_call" | custom-call | tf_op jit(solution)/shard_map/pallas_call | solution.py:502
  36.4 1.2 %slice.7 = f32[1,1]{1,0:T(1,128)} slice(f32[8,64]{1,0:T(8,128)} %shard_map.113), slice={[3:4], [0:1]} | slice | bytes 8 | tf_op jit(solution)/shard_map/slice | solution.py:557
  37.6 1.3 %slice.6 = f32[3,64]{1,0:T(4,128)} slice(f32[8,64]{1,0:T(8,128)} %shard_map.113), slice={[0:3], [0:64]} | slice | bytes 1536 | tf_op jit(solution)/shard_map/slice | solution.py:557

commit v5 on v4

--- a/solution.py
+++ b/solution.py
@@ -65,7 +65,7 @@
 def kernel(
     columns, rows, sizes,
     pos_in, feat_in, send_in, src_in, dst_in, count_in, we_in, wv_in, wu_in, wo_in,
-    out_ref,
+    forces_ref, energy_ref,
     pos_ref, feat_ref, send_ref, src_ref, dst_ref, count_ref, we_ref, wv_ref, wu_ref, wo_ref,
     pay, table, ah, al, oh, vh, vl, row, value, gain_cut, df, dradial_map, ddb, lhs, own_weights, flat, kept, folded,
     uth, utl, embs, gsrc, gbuf, ebuf,
@@ -138,7 +138,16 @@
     e3 = split3(jnp.concatenate([exported, jnp.zeros((128, 128 - ATOMS), F32)], axis=1))
     st4_tall = jnp.concatenate([st4, jnp.zeros((128 - ATOMS, 128), BF16)], axis=0)
     payload = (dot(e3[2], st4_tall) + dot(e3[1], st4_tall)) + dot(e3[0], st4_tall)
-    pay[...] = payload.T[0:GHOST, :]
+    lane_group = lax.broadcasted_iota(jnp.int32, (16, 128), 1) >> 5
+
+    def by_group(parts):
+        result = parts[0]
+        for q in range(1, len(parts)):
+            result = jnp.where(lane_group[0 : result.shape[0]] == q, parts[q], result)
+        return result
+
+    pay[0:16] = by_group([payload[16 * q : 16 * q + 16] for q in range(4)])
+    pay[16:17] = by_group([payload[C + i : C + i + 1] for i in range(3)])
 
     inner = jnp.logical_and(b > 0, b < rows - 1)
     pl.semaphore_wait(barrier, greeted + jnp.where(inner, 8, 5))
@@ -236,18 +245,29 @@
 
     def blank(g):
         for i in range(*SPANS[g]):
-            table[i] = jnp.zeros((GHOST, 128), F32)
+            table[i] = jnp.zeros((17, 128), F32)
             gbuf[i] = jnp.zeros((8, 128), F32)
 
     each_group(lambda g: ghost_group(g).wait_recv(), blank)
 
-    ghosts = jnp.concatenate([table[0:4].reshape(128, 128).T, table[4:8].reshape(128, 128).T], axis=1)
+    def turned(x, groups):
+        cut = 128 - 32 * (groups % 4)
+        return x if groups % 4 == 0 else jnp.concatenate([x[:, cut:], x[:, :cut]], axis=1)
+
+    channels, coords = [[], [], [], []], [[], [], []]
+    for t in range(2):
+        held = [table[4 * t + i] for i in range(4)]
+        for q in range(4):
+            around = [turned(held[i], i - q) for i in range(4)]
+            channels[q].append(by_group([x[0:16] for x in around]))
+            if q < 3:
+                coords[q].append(by_group([x[16:17] for x in around]))
+    ghosts = jnp.concatenate([jnp.concatenate(x, axis=1) for x in channels], axis=0)
     own_pos = jnp.concatenate([pos, jnp.zeros((3, 64), F32)], axis=1)
     diff = []
     for i in range(3):
-        at_ghost = ghosts[C + i : C + i + 1, :]
         mine = own_pos[i : i + 1, :]
-        at_src = pick_lane([at_ghost[:, 0:128], at_ghost[:, 128:256], mine], slot)
+        at_src = pick_lane(coords[i] + [mine], slot)
         if i < 2:
             at_src = at_src + (ox, oy)[i]
         diff.append(at_src - pick_lane([mine], dst))
@@ -278,7 +298,7 @@
 
     loop(8, map_edges)
 
-    emb_hi, emb_lo = split(jnp.concatenate([ghosts[0:C, :], own_src, own_dst], axis=1))
+    emb_hi, emb_lo = split(jnp.concatenate([ghosts, own_src, own_dst], axis=1))
     embs[...] = jnp.concatenate(
         [jnp.concatenate([emb_hi, wr4], axis=1), jnp.concatenate([emb_lo, jnp.zeros((C, 128), BF16)], axis=1)], axis=0)
     order = (lax.broadcasted_iota(jnp.int32, (NB, TILE), 0) + 1).astype(F32)
@@ -474,17 +494,15 @@
         force_group(g).wait_send()
 
     each_group(forces_in)
-    lane_group = lax.broadcasted_iota(jnp.int32, (8, 128), 1) >> 5
     acc = jnp.zeros((8, 128), F32)
     for k in range(8):
-        acc = acc + jnp.where(lane_group == PLACE[7 - k] % 4, gbuf[PLACE[k]], 0.0)
+        acc = acc + jnp.where(lane_group[0:8] == PLACE[7 - k] % 4, gbuf[PLACE[k]], 0.0)
     acc_low = acc - acc.astype(BF16).astype(F32)
     returned = dot_t(jnp.concatenate([acc, acc_low], axis=0).astype(BF16), st4)
-    forces = -(at_own + returned[0:8] + returned[8:16])
+    forces_ref[...] = -(at_own + returned[0:8] + returned[8:16])[0:3]
 
     total = energy_in(2)
-    energy = jnp.sum(jnp.sum(total, axis=0, keepdims=True), axis=1, keepdims=True)
-    out_ref[...] = jnp.where(lax.broadcasted_iota(jnp.int32, (8, ATOMS), 0) == 3, energy, forces)
+    energy_ref[...] = jnp.sum(jnp.sum(total, axis=0, keepdims=True), axis=1, keepdims=True)
     energy_group(2).wait_send()
 
 
@@ -499,11 +517,11 @@
 
         vmem = pl.BlockSpec(memory_space=pltpu.VMEM)
         anywhere = pl.BlockSpec(memory_space=pl.ANY)
-        out = pl.pallas_call(
+        forces, energy = pl.pallas_call(
             body,
-            out_shape=jax.ShapeDtypeStruct((8, ATOMS), F32),
+            out_shape=(jax.ShapeDtypeStruct((3, ATOMS), F32), jax.ShapeDtypeStruct((1, 1), F32)),
             in_specs=[anywhere] * 10,
-            out_specs=vmem,
+            out_specs=(vmem, vmem),
             scratch_shapes=[
                 pltpu.VMEM((3, ATOMS), F32),
                 pltpu.VMEM((C, ATOMS), BF16),
@@ -515,8 +533,8 @@
                 pltpu.VMEM((LAYERS, C, 3 * C), F32),
                 pltpu.VMEM((LAYERS, C, 4 * C), F32),
                 pltpu.VMEM((1, C), F32),
-                pltpu.VMEM((GHOST, 128), F32),
-                pltpu.VMEM((8, GHOST, 128), F32),
+                pltpu.VMEM((17, 128), F32),
+                pltpu.VMEM((8, 17, 128), F32),
                 pltpu.VMEM((768, EDGES), BF16),
                 pltpu.VMEM((512, EDGES), BF16),
                 pltpu.VMEM((512, EDGES), BF16),
@@ -554,7 +572,7 @@
             positions, features, send_list.reshape(1, GHOST), edge_src.reshape(8, 128), edge_dst.reshape(8, 128),
             edge_count.reshape(1, 1), w_embed.T, w_env, jnp.swapaxes(w_update, 1, 2), w_out.reshape(1, C),
         )
-        return out[0:3], out[3, 0]
+        return forces, energy.reshape(())
 
     placed = (
         P(None, ("gx", "gy")), P(None, ("gx", "gy")), P(("gx", "gy")), P(("gx", "gy")), P(("gx", "gy")),

time: 39 us -> 39.4 us (1.010)
  between operations: 1.29 us -> 3.06 us
  local copies, waits for them, and re-layouts: 2.45 us -> 1.22 us
  Pallas kernels: 35.1 us -> 34.6 us
    slice x2 -> x0, local copies, waits for them, and re-layouts: 2.45 us -> none  [per_device(): return (out[0:3], out[3, 0])]
    unnamed x0 -> x3, local copies, waits for them, and re-layouts: none -> 1.22 us
    pallas_call x1, Pallas kernels: 35.1 us -> 34.6 us  [per_device(): pl.pallas_call(body, out_shape=(jax.ShapeDtypeStruct((3, ATOMS), F32), ja...]
where the time goes in v5:
time: 39.4 us; the launch traced here: 38.9 us
  Pallas kernels  34.6 us (88%)
  between operations  3.06 us (8%)
  local copies, waits for them, and re-layouts  1.22 us (3%)
    pallas_call x1, Pallas kernels, per_device(): pl.pallas_call(body, out_shape=(jax.ShapeDtypeStruct((3, ATOMS), F32), ja...  34.6 us
    unnamed x3, local copies, waits for them, and re-layouts  1.22 us

profile of v5, /device:TPU:1, one launch (start us, length us, event | category | flops | bytes accessed | tf_op | source)
XLA Modules:
  0.0 38.9 jit_solution(6303902185130383101)
XLA Ops:
  1.3 34.6 %shard_map.113 = (f32[3,64]{1,0:T(4,128)}, f32[1,1]{1,0:T(1,128)}) custom-call(f32[3,64]{1,0:T(4,128)} %refs_0_.1, bf16[64,64]{1,0:T(8,128)(2,1)} %refs_1_.1, s32[1,32]{1,0:T(1,128)} %bitcast.13, s32[8,128]{1,0:T(8,128)} %bitcast.11, s32[8,128]{1,0:T(8,128)} %bitcast.12, s32[1,1]{1,0:T(1,128)} %bitcast.8.refs_5_, f32[64,136]{1,0:T(8,128)} %bitcast.10, ...), custom_call_target="tpu_custom_call" | custom-call | tf_op jit(solution)/shard_map/pallas_call | solution.py:520
  35.9 0.0 copy-start
  35.9 0.6 %copy-done = f32[3,64]{1,0:T(4,128)S(1)} copy-done((f32[3,64]{1,0:T(4,128)S(1)}, f32[3,64]{1,0:T(4,128)}, u32[]{:S(2)}) %copy-start) | copy-done | bytes 792
  36.6 0.6 %copy.15 = f32[3,64]{1,0:T(4,128)} copy(f32[3,64]{1,0:T(4,128)S(1)} %copy-done) | data formatting | bytes 1536
Async XLA Ops:
  35.9 0.7 %copy-start = (f32[3,64]{1,0:T(4,128)S(1)}, f32[3,64]{1,0:T(4,128)}, u32[]{:S(2)}) copy-start(f32[3,64]{1,0:T(4,128)} %get-tuple-element.8) | copy-start | bytes 2308

commit v6 on v5

--- a/solution.py
+++ b/solution.py
@@ -202,7 +202,7 @@
     step_y = (oy * (1.0 / WIDTH)).astype(jnp.int32)
     reach = jnp.logical_and(b + step_y >= 0, b + step_y < rows)
     place = lax.broadcasted_iota(jnp.int32, (8, 128), 0) * 128 + lax.broadcasted_iota(jnp.int32, (8, 128), 1)
-    live = jnp.where(jnp.logical_and(place < count_ref[...], reach), 1.0, 0.0)
+    live = jnp.where(jnp.logical_and(place < count_ref[0], reach), 1.0, 0.0)
     put_row(LIVE, live)
     slot = jnp.where(ghost, block_place * GHOST + (src & (GHOST - 1)), src + 8 * GHOST)
     def one_hot(j):
@@ -502,7 +502,7 @@
     forces_ref[...] = -(at_own + returned[0:8] + returned[8:16])[0:3]
 
     total = energy_in(2)
-    energy_ref[...] = jnp.sum(jnp.sum(total, axis=0, keepdims=True), axis=1, keepdims=True)
+    energy_ref[...] = jnp.sum(total, axis=0, keepdims=True)
     energy_group(2).wait_send()
 
 
@@ -519,7 +519,7 @@
         anywhere = pl.BlockSpec(memory_space=pl.ANY)
         forces, energy = pl.pallas_call(
             body,
-            out_shape=(jax.ShapeDtypeStruct((3, ATOMS), F32), jax.ShapeDtypeStruct((1, 1), F32)),
+            out_shape=(jax.ShapeDtypeStruct((3, ATOMS), F32), jax.ShapeDtypeStruct((1, 128), F32)),
             in_specs=[anywhere] * 10,
             out_specs=(vmem, vmem),
             scratch_shapes=[
@@ -528,7 +528,7 @@
                 pltpu.VMEM((1, GHOST), jnp.int32),
                 pltpu.VMEM((8, 128), jnp.int32),
                 pltpu.VMEM((8, 128), jnp.int32),
-                pltpu.VMEM((1, 1), jnp.int32),
+                pltpu.SMEM((1,), jnp.int32),
                 pltpu.VMEM((C, 2 * C + NB), F32),
                 pltpu.VMEM((LAYERS, C, 3 * C), F32),
                 pltpu.VMEM((LAYERS, C, 4 * C), F32),
@@ -570,9 +570,9 @@
             ),
         )(
             positions, features, send_list.reshape(1, GHOST), edge_src.reshape(8, 128), edge_dst.reshape(8, 128),
-            edge_count.reshape(1, 1), w_embed.T, w_env, jnp.swapaxes(w_update, 1, 2), w_out.reshape(1, C),
+            edge_count, w_embed.T, w_env, jnp.swapaxes(w_update, 1, 2), w_out.reshape(1, C),
         )
-        return forces, energy.reshape(())
+        return forces, jnp.sum(energy)
 
     placed = (
         P(None, ("gx", "gy")), P(None, ("gx", "gy")), P(("gx", "gy")), P(("gx", "gy")), P(("gx", "gy")),

time: 39.4 us -> 38.2 us (0.970)
  between operations: 3.06 us -> 1.3 us
  other arithmetic: 0 us -> 0.6 us
    reduce_sum x0 -> x1, other arithmetic: none -> 0.6 us  [per_device(): return (forces, jnp.sum(energy))]
    unnamed x3 -> x5, local copies, waits for them, and re-layouts: 1.22 us -> 1.27 us
where the time goes in v6:
time: 38.2 us; the launch traced here: 37.7 us
  Pallas kernels  34.6 us (91%)
  between operations  1.3 us (3%)
  local copies, waits for them, and re-layouts  1.27 us (3%)
  other arithmetic  0.6 us (2%)
    pallas_call x1, Pallas kernels, per_device(): pl.pallas_call(body, out_shape=(jax.ShapeDtypeStruct((3, ATOMS), F32), ja...  34.6 us
    unnamed x5, local copies, waits for them, and re-layouts  1.27 us

profile of v6, /device:TPU:1, one launch (start us, length us, event | category | flops | bytes accessed | tf_op | source)
XLA Modules:
  0.0 37.7 jit_solution(9643619357923422571)
XLA Ops:
  1.3 34.6 %shard_map.113 = (f32[3,64]{1,0:T(4,128)}, f32[1,128]{1,0:T(1,128)}) custom-call(f32[3,64]{1,0:T(4,128)} %refs_0_.1, bf16[64,64]{1,0:T(8,128)(2,1)} %refs_1_.1, s32[1,32]{1,0:T(1,128)} %bitcast.10, s32[8,128]{1,0:T(8,128)} %bitcast.8, s32[8,128]{1,0:T(8,128)} %bitcast.9, s32[1]{0:T(128)S(6)} %copy.13.refs_5_, f32[64,136]{1,0:T(8,128)} %bitcast.7, ...), custom_call_target="tpu_custom_call" | custom-call | tf_op jit(solution)/shard_map/pallas_call | solution.py:520
  35.9 0.0 copy-start.1
  35.9 0.6 %copy-done.1 = f32[1,128]{1,0:T(1,128)S(1)} copy-done((f32[1,128]{1,0:T(1,128)S(1)}, f32[1,128]{1,0:T(1,128)}, u32[]{:S(2)}) %copy-start.1) | copy-done | bytes 536
  36.5 0.0 copy-start
  36.5 0.6 %reduce_sum.9 = f32[]{:T(128)} reduce(f32[1,128]{1,0:T(1,128)S(1)} %copy-done.1, f32[]{:T(128)} %constant.0.clone.1), dimensions={0,1}, to_apply=%region_0.0 | reduce | flops 127 | bytes 520 | tf_op jit(solution)/shard_map/reduce_sum | solution.py:575
  37.1 0.1 copy-done
  37.2 0.6 %copy.14 = f32[3,64]{1,0:T(4,128)} copy(f32[3,64]{1,0:T(4,128)S(1)} %copy-done) | data formatting | bytes 1536
Async XLA Ops:
  35.9 0.6 %copy-start.1 = (f32[1,128]{1,0:T(1,128)S(1)}, f32[1,128]{1,0:T(1,128)}, u32[]{:S(2)}) copy-start(f32[1,128]{1,0:T(1,128)} %get-tuple-element.5) | copy-start | bytes 1540
  36.5 0.7 %copy-start = (f32[3,64]{1,0:T(4,128)S(1)}, f32[3,64]{1,0:T(4,128)}, u32[]{:S(2)}) copy-start(f32[3,64]{1,0:T(4,128)} %get-tuple-element.8) | copy-start | bytes 2308

commit v7 on v6

--- a/solution.py
+++ b/solution.py
@@ -566,7 +566,7 @@
                 pltpu.SemaphoreType.DMA((3,)),
             ],
             compiler_params=pltpu.CompilerParams(
-                collective_id=0, has_side_effects=True, vmem_limit_bytes=60 * 1024 * 1024
+                collective_id=0, has_side_effects=True, vmem_limit_bytes=55216 * 1024
             ),
         )(
             positions, features, send_list.reshape(1, GHOST), edge_src.reshape(8, 128), edge_dst.reshape(8, 128),

time: 38.2 us -> 37.4 us (0.979)
  Pallas kernels: 34.6 us -> 33.8 us
    pallas_call x1, Pallas kernels: 34.6 us -> 33.8 us  [per_device(): pl.pallas_call(body, out_shape=(jax.ShapeDtypeStruct((3, ATOMS), F32), ja...]
where the time goes in v7:
time: 37.4 us; the launch traced here: 37 us
  Pallas kernels  33.8 us (90%)
  between operations  1.3 us (3%)
  local copies, waits for them, and re-layouts  1.23 us (3%)
  other arithmetic  0.6 us (2%)
    pallas_call x1, Pallas kernels, per_device(): pl.pallas_call(body, out_shape=(jax.ShapeDtypeStruct((3, ATOMS), F32), ja...  33.8 us
    unnamed x5, local copies, waits for them, and re-layouts  1.23 us

profile of v7, /device:TPU:1, one launch (start us, length us, event | category | flops | bytes accessed | tf_op | source)
XLA Modules:
  0.0 37.0 jit_solution(16081489596253575445)
XLA Ops:
  1.3 0.0 copy-start
  1.3 0.0 copy-start.1
  1.3 0.6 %copy-done = s32[32]{0:T(128)S(1)} copy-done((s32[32]{0:T(128)S(1)}, s32[32]{0:T(128)}, u32[]{:S(2)}) %copy-start) | copy-done | bytes 152
  1.9 0.0 copy-done.1
  2.0 33.8 %shard_map.113 = (f32[3,64]{1,0:T(4,128)S(1)}, f32[1,128]{1,0:T(1,128)S(1)}) custom-call(f32[3,64]{1,0:T(4,128)} %refs_0_.1, bf16[64,64]{1,0:T(8,128)(2,1)} %refs_1_.1, s32[1,32]{1,0:T(1,128)S(1)} %bitcast.6, s32[8,128]{1,0:T(8,128)} %bitcast.10, s32[8,128]{1,0:T(8,128)} %bitcast.11, s32[1]{0:T(128)S(6)} %copy.13.refs_5_, f32[64,136]{1,0:T(8,128)} %bitcast.9, ...), custom_call_target="tpu_custom_call" | custom-call | tf_op jit(solution)/shard_map/pallas_call | solution.py:520
  35.8 0.6 %reduce_sum.9 = f32[]{:T(128)} reduce(f32[1,128]{1,0:T(1,128)S(1)} %get-tuple-element.5, f32[]{:T(128)} %constant.0.clone.1), dimensions={0,1}, to_apply=%region_0.0 | reduce | flops 127 | bytes 520 | tf_op jit(solution)/shard_map/reduce_sum | solution.py:575
  36.4 0.6 %copy.14 = f32[3,64]{1,0:T(4,128)} copy(f32[3,64]{1,0:T(4,128)S(1)} %get-tuple-element.8) | data formatting | bytes 1536
Async XLA Ops:
  1.3 0.7 %copy-start = (s32[32]{0:T(128)S(1)}, s32[32]{0:T(128)}, u32[]{:S(2)}) copy-start(s32[32]{0:T(128)} %param.12) | copy-start | bytes 388
  1.3 0.7 %copy-start.1 = (f32[64]{0:T(128)S(1)}, f32[64]{0:T(128)}, u32[]{:S(2)}) copy-start(f32[64]{0:T(128)} %param.19) | copy-start | bytes 772

commit v8 on v7

--- a/solution.py
+++ b/solution.py
@@ -435,10 +435,10 @@
     energy_out(0, folded[:, 0:128] + folded[:, 128:256])
     mix(2, 64)
     tiles(back_first)
+    energy_out(1, energy_in(0))
     back_map(0)
     mix(3, 192)
     back_map(128)
-    energy_out(1, energy_in(0))
 
     def back_embed(lanes):
         g = df[:, lanes] + spread(lanes)

time: 37.4 us -> 38.1 us (1.019)
  Pallas kernels: 33.8 us -> 34.9 us
    pallas_call x1, Pallas kernels: 33.8 us -> 34.9 us  [per_device(): pl.pallas_call(body, out_shape=(jax.ShapeDtypeStruct((3, ATOMS), F32), ja...]
where the time goes in v8:
time: 38.1 us; the launch traced here: 38 us
  Pallas kernels  34.9 us (92%)
  between operations  1.3 us (3%)
  local copies, waits for them, and re-layouts  1.23 us (3%)
  other arithmetic  0.6 us (2%)
    pallas_call x1, Pallas kernels, per_device(): pl.pallas_call(body, out_shape=(jax.ShapeDtypeStruct((3, ATOMS), F32), ja...  34.9 us
    unnamed x5, local copies, waits for them, and re-layouts  1.23 us

profile of v8, /device:TPU:1, one launch (start us, length us, event | category | flops | bytes accessed | tf_op | source)
XLA Modules:
  0.0 38.0 jit_solution(17515822311550158106)
XLA Ops:
  1.3 0.0 copy-start
  1.3 0.0 copy-start.1
  1.3 0.6 %copy-done = s32[32]{0:T(128)S(1)} copy-done((s32[32]{0:T(128)S(1)}, s32[32]{0:T(128)}, u32[]{:S(2)}) %copy-start) | copy-done | bytes 152
  1.9 0.0 copy-done.1
  2.0 34.9 %shard_map.113 = (f32[3,64]{1,0:T(4,128)S(1)}, f32[1,128]{1,0:T(1,128)S(1)}) custom-call(f32[3,64]{1,0:T(4,128)} %refs_0_.1, bf16[64,64]{1,0:T(8,128)(2,1)} %refs_1_.1, s32[1,32]{1,0:T(1,128)S(1)} %bitcast.6, s32[8,128]{1,0:T(8,128)} %bitcast.10, s32[8,128]{1,0:T(8,128)} %bitcast.11, s32[1]{0:T(128)S(6)} %copy.13.refs_5_, f32[64,136]{1,0:T(8,128)} %bitcast.9, ...), custom_call_target="tpu_custom_call" | custom-call | tf_op jit(solution)/shard_map/pallas_call | solution.py:520
  36.8 0.6 %reduce_sum.9 = f32[]{:T(128)} reduce(f32[1,128]{1,0:T(1,128)S(1)} %get-tuple-element.5, f32[]{:T(128)} %constant.0.clone.1), dimensions={0,1}, to_apply=%region_0.0 | reduce | flops 127 | bytes 520 | tf_op jit(solution)/shard_map/reduce_sum | solution.py:575
  37.4 0.6 %copy.14 = f32[3,64]{1,0:T(4,128)} copy(f32[3,64]{1,0:T(4,128)S(1)} %get-tuple-element.8) | data formatting | bytes 1536
Async XLA Ops:
  1.3 0.7 %copy-start = (s32[32]{0:T(128)S(1)}, s32[32]{0:T(128)}, u32[]{:S(2)}) copy-start(s32[32]{0:T(128)} %param.12) | copy-start | bytes 388
  1.3 0.7 %copy-start.1 = (f32[64]{0:T(128)S(1)}, f32[64]{0:T(128)}, u32[]{:S(2)}) copy-start(f32[64]{0:T(128)} %param.19) | copy-start | bytes 772

commit v9 on v7

--- a/solution.py
+++ b/solution.py
@@ -23,7 +23,7 @@
 F32 = jnp.float32
 BF16 = jnp.bfloat16
 MESH = pl.DeviceIdType.MESH
-TILE = 256
+TILE = 512
 CUT, LIVE, UX, UY, UZ, INV, DIST, GAIN, BEND, SLOPE, DCUT = 0, 1, 2, 3, 4, 5, 6, 7, 8, 9, 10
 
 
@@ -432,7 +432,7 @@
     mix(1, 0)
     weigh(3)
     tiles(turn)
-    energy_out(0, folded[:, 0:128] + folded[:, 128:256])
+    energy_out(0, sum(folded[:, 128 * j : 128 * (j + 1)] for j in range(TILE // 128)))
     mix(2, 64)
     tiles(back_first)
     back_map(0)

time: 37.4 us -> 37.4 us (level)
  no operation moved by 1% of the time
where the time goes in v9:
time: 37.4 us; the launch traced here: 36.9 us
  Pallas kernels  33.8 us (90%)
  between operations  1.3 us (3%)
  local copies, waits for them, and re-layouts  1.23 us (3%)
  other arithmetic  0.6 us (2%)
    pallas_call x1, Pallas kernels, per_device(): pl.pallas_call(body, out_shape=(jax.ShapeDtypeStruct((3, ATOMS), F32), ja...  33.8 us
    unnamed x5, local copies, waits for them, and re-layouts  1.23 us

profile of v9, /device:TPU:1, one launch (start us, length us, event | category | flops | bytes accessed | tf_op | source)
XLA Modules:
  0.0 36.9 jit_solution(9733915492502634525)
XLA Ops:
  1.3 0.0 copy-start
  1.3 0.0 copy-start.1
  1.3 0.6 %copy-done = s32[32]{0:T(128)S(1)} copy-done((s32[32]{0:T(128)S(1)}, s32[32]{0:T(128)}, u32[]{:S(2)}) %copy-start) | copy-done | bytes 152
  1.9 0.0 copy-done.1
  2.0 33.8 %shard_map.113 = (f32[3,64]{1,0:T(4,128)S(1)}, f32[1,128]{1,0:T(1,128)S(1)}) custom-call(f32[3,64]{1,0:T(4,128)} %refs_0_.1, bf16[64,64]{1,0:T(8,128)(2,1)} %refs_1_.1, s32[1,32]{1,0:T(1,128)S(1)} %bitcast.6, s32[8,128]{1,0:T(8,128)} %bitcast.10, s32[8,128]{1,0:T(8,128)} %bitcast.11, s32[1]{0:T(128)S(6)} %copy.13.refs_5_, f32[64,136]{1,0:T(8,128)} %bitcast.9, ...), custom_call_target="tpu_custom_call" | custom-call | tf_op jit(solution)/shard_map/pallas_call | solution.py:520
  35.8 0.6 %reduce_sum.9 = f32[]{:T(128)} reduce(f32[1,128]{1,0:T(1,128)S(1)} %get-tuple-element.5, f32[]{:T(128)} %constant.0.clone.1), dimensions={0,1}, to_apply=%region_0.0 | reduce | flops 127 | bytes 520 | tf_op jit(solution)/shard_map/reduce_sum | solution.py:575
  36.4 0.6 %copy.14 = f32[3,64]{1,0:T(4,128)} copy(f32[3,64]{1,0:T(4,128)S(1)} %get-tuple-element.8) | data formatting | bytes 1536
Async XLA Ops:
  1.3 0.7 %copy-start = (s32[32]{0:T(128)S(1)}, s32[32]{0:T(128)}, u32[]{:S(2)}) copy-start(s32[32]{0:T(128)} %param.12) | copy-start | bytes 388
  1.3 0.7 %copy-start.1 = (f32[64]{0:T(128)S(1)}, f32[64]{0:T(128)}, u32[]{:S(2)}) copy-start(f32[64]{0:T(128)} %param.19) | copy-start | bytes 772
